TPU v7x, 256 devices: a whole 4x4x8 slice. The times are simulated.
256 devices in a mesh: row: 32 (over z_lo, y, core), col: 8 (over x, z_hi).
Axes of the slice: x: 4, y: 4, z: 8 (z_hi: 2, z_lo: 4; z = z_hi * 4 + z_lo), core: 2. Of those that a mesh axis runs over, the one named last changes fastest.
Arguments:
- blocks: bfloat16 [3072, 512, 512], P(('row', 'col')), as said below
- block_rows: int32 [3072], P(('row', 'col')), may hold values from 0 to 511, as said below
- block_cols: int32 [3072], P(('row', 'col')), may hold values from 0 to 511
- inter_counts: int32 [256], P(('row', 'col')), may hold values from 1 to 8, as said below
- keep_mask: int32 [262144], P('row'), may hold values 0 or 1
Outputs:
- bias_final: float32 [262144], P('row')
- balance: float32 [262144], P('row')
Inputs may be any that keep to these rules, and one draw needn't show every extreme that they name: `block_rows`: slots of device row index r have block rows from r * 16 to (r + 1) * 16 - 1. The band slots of the devices sharing r hold, in some order, for each such block row i the blocks (i, i) and (i, i - 1), where block row 0's second block is (0, 0) again. Inter-region blocks have block columns not below their block rows. `inter_counts`: some device has all 8 inter-region slots live. `blocks`: positive counts.
All inputs are finite; a program needn't handle non-finite values. No bound on the sum of `keep_mask` on one device may be relied on, other than what follows from the above.
Results may differ from a plain program's by a relative error of at most 0.0004.
Values sent between devices are 32-bit elements; how exact they have to be, the bound alone decides.
A program may use at most 64 MiB of HBM per device.

v0:
```python
import jax
import jax.numpy as jnp
from jax import lax
from jax.sharding import PartitionSpec as P

IR_MAX = 8
SWEEPS = 3


def split_pair(values):
    upper = values.astype(jnp.bfloat16)
    lower = (values - upper.astype(jnp.float32)).astype(jnp.bfloat16)
    return jnp.stack([upper, lower], axis=-1)


def body(blocks, block_rows, block_cols, inter_counts, keep_mask):
    slot_count = blocks.shape[0]
    block_width = blocks.shape[1]
    seg_len = keep_mask.shape[0]
    rows_here = seg_len // block_width
    total_rows = rows_here * lax.axis_size("row")
    row_base = lax.axis_index("row") * rows_here
    slot_ids = jnp.arange(slot_count)
    band_slots = slot_count - IR_MAX
    active = ((slot_ids < band_slots) | (slot_ids - band_slots < inter_counts[0])).astype(
        jnp.float32
    )
    pick_cols = (block_cols[:, None] == jnp.arange(total_rows)[None, :]).astype(jnp.float32)
    pick_rows = ((block_rows - row_base)[:, None] == jnp.arange(rows_here)[None, :]).astype(
        jnp.float32
    )
    mask_float = keep_mask.astype(jnp.float32)
    highest = lax.Precision.HIGHEST
    bias_now = jnp.ones((seg_len,), jnp.float32)
    balance = jnp.zeros((seg_len,), jnp.float32)
    for sweep_index in range(SWEEPS):
        weights = mask_float / bias_now
        w_full = lax.all_gather(weights, "row", axis=0, tiled=True)
        w_table = w_full.reshape(total_rows, block_width)
        w_cols = jnp.dot(pick_cols, w_table, precision=highest)
        own_rows = lax.dynamic_slice_in_dim(w_table, row_base, rows_here, 0)
        w_rows = jnp.dot(pick_rows, own_rows, precision=highest)
        pair_cols = split_pair(w_cols)
        pair_rows = split_pair(w_rows)
        row_pair = jnp.einsum("kab,kbt->kat", blocks, pair_cols, preferred_element_type=jnp.float32)
        col_pair = jnp.einsum("kab,kat->kbt", blocks, pair_rows, preferred_element_type=jnp.float32)
        row_part = (row_pair[:, :, 0] + row_pair[:, :, 1]) * active[:, None]
        col_part = (col_pair[:, :, 0] + col_pair[:, :, 1]) * active[:, None]
        col_total = jnp.dot(pick_cols.T, col_part, precision=highest)
        row_total = jnp.dot(pick_rows.T, row_part, precision=highest)
        col_total, row_total = (col_total, row_total)
        segment_sums = lax.psum_scatter(
            col_total.reshape(-1), "row", scatter_dimension=0, tiled=True
        ) + row_total.reshape(-1)
        summed = lax.psum(segment_sums, "col")
        bin_sums = weights * summed
        kept_total, kept_count = lax.psum(
            (jnp.sum(bin_sums * mask_float), jnp.sum(mask_float)), "row"
        )
        mean_sum = kept_total / kept_count
        bias_now = jnp.where(keep_mask > 0, bias_now * bin_sums / mean_sum, bias_now)
        balance = bin_sums / mean_sum
    return (bias_now, balance)


def solution(mesh):
    return jax.shard_map(
        body,
        mesh=mesh,
        in_specs=(
            P(("row", "col"), None, None),
            P(("row", "col")),
            P(("row", "col")),
            P(("row", "col")),
            P("row"),
        ),
        out_specs=(P("row"), P("row")),
        check_vma=False,
    )
```

profile of v0, /device:TPU:1, one launch (start us, length us, event | category | flops | bytes accessed | tf_op | source)
XLA Modules:
  0.0 1407.5 jit_solution(3411200096953311003)
XLA Ops:
  7.2 0.0 copy-start.2
  7.2 0.0 all-gather.4.cloned.1.call-start
  7.2 1.4 convert_element_type.66
  8.6 0.0 all-gather.4.cloned.1.call-update
  8.6 0.0 all-reduce.8.cloned.1.call-start
  9.3 0.7 broadcast_subtract_fusion
  10.0 63.6 %all-gather.4.cloned.1.call-done = f32[262144]{0:T(1024)} async-done(((f32[8192]{0:T(1024)}), f32[262144]{0:T(1024)}) %all-gather.4.cloned.1.call-update) | async-done | bytes 1048592 | tf_op jit(solution)/shard_map/all_gather | solution.py:38
  73.6 1.4 reshape.48
  75.0 0.2 convert_bitcast_fusion.5
  75.2 3.7 convolution_bitcast_fusion.3
  79.0 0.0 copy-done.2
  79.0 0.7 convolution_bitcast_fusion.2
  79.7 1.3 copy.30
  81.0 0.0 all-reduce.8.cloned.1.call-update
  81.0 0.0 all-gather.6.cloned.1.call-start
  81.1 0.0 copy-done.3
  81.1 0.6 dynamic-slice
  82.3 0.5 convert_bitcast_fusion.4
  82.8 4.5 fusion.38
  87.3 0.3 convolution_bitcast_fusion.6
  87.6 269.9 %all-reduce.8.cloned.1.call-done = f32[262144]{0:T(1024)} async-done(((f32[262144]{0:T(1024)}), f32[262144]{0:T(1024)}) %all-reduce.8.cloned.1.call-update) | async-done | bytes 1048592
  357.6 0.8 dynamic-slice_add_fusion.2
  358.3 44.3 %psum.55 = f32[8192]{0:T(1024)S(1)} all-reduce(f32[8192]{0:T(1024)S(1)} %dynamic-slice_add_fusion.2), channel_id=1, replica_groups=mesh['row'=32,'col'=8] {'col'}, use_global_device_ids=true, to_apply=%region_1.0 | all-reduce | flops 8192 | bytes 65536 | tf_op jit(solution)/shard_map/psum | solution.py:55
  402.6 0.6 convert_reduce_fusion
  403.2 77.3 %all-reduce.3 = (f32[]{:T(128)}, f32[]{:T(128)}) all-reduce(f32[]{:T(128)} %get-tuple-element.3, f32[]{:T(128)} %get-tuple-element.2), channel_id=1, replica_groups=mesh['row'=32,'col'=8] {'row'}, use_global_device_ids=true, to_apply=%region_3.0 | all-reduce | flops 2 | bytes 16 | tf_op jit(solution)/shard_map/psum | solution.py:57
  481.8 0.6 fusion.59
  482.4 0.0 all-gather.6.cloned.1.call-update
  482.5 0.0 all-reduce.10.cloned.1.call-start
  482.5 50.2 %all-gather.6.cloned.1.call-done = f32[262144]{0:T(1024)} async-done(((f32[8192]{0:T(1024)}), f32[262144]{0:T(1024)}) %all-gather.6.cloned.1.call-update) | async-done | bytes 1048592 | tf_op jit(solution)/shard_map/all_gather | solution.py:38
  532.7 1.4 reshape.51
  534.1 0.2 convert_bitcast_fusion.3
  534.4 3.7 fusion.36
  538.1 0.7 convolution_bitcast_fusion.1
  538.8 1.3 copy.32
  540.1 0.0 all-reduce.10.cloned.1.call-update
  540.1 0.0 all-gather.8.cloned.1.call-start
  540.2 0.5 convert_bitcast_fusion.2
  540.6 4.5 fusion.34
  545.2 0.3 convolution_bitcast_fusion.5
  545.5 271.2 %all-reduce.10.cloned.1.call-done = f32[262144]{0:T(1024)} async-done(((f32[262144]{0:T(1024)}), f32[262144]{0:T(1024)}) %all-reduce.10.cloned.1.call-update) | async-done | bytes 1048592
  816.7 0.8 dynamic-slice_add_fusion.1
  817.4 44.3 %psum.58 = f32[8192]{0:T(1024)S(1)} all-reduce(f32[8192]{0:T(1024)S(1)} %dynamic-slice_add_fusion.1), channel_id=1, replica_groups=mesh['row'=32,'col'=8] {'col'}, use_global_device_ids=true, to_apply=%region_7.8 | all-reduce | flops 8192 | bytes 65536 | tf_op jit(solution)/shard_map/psum | solution.py:55
  861.7 0.6 multiply_reduce_fusion.1
  862.3 77.3 %psum.59 = f32[]{:T(128)} all-reduce(f32[]{:T(128)} %multiply_reduce_fusion.1), channel_id=1, replica_groups=mesh['row'=32,'col'=8] {'row'}, use_global_device_ids=true, to_apply=%region_9.10 | all-reduce | flops 1 | bytes 8 | tf_op jit(solution)/shard_map/psum | solution.py:57
  940.9 0.6 convert_divide_fusion
  941.5 0.0 all-gather.8.cloned.1.call-update
  941.6 0.0 all-reduce.12.cloned.1.call-start
  941.6 50.2 %all-gather.8.cloned.1.call-done = f32[262144]{0:T(1024)} async-done(((f32[8192]{0:T(1024)}), f32[262144]{0:T(1024)}) %all-gather.8.cloned.1.call-update) | async-done | bytes 1048592 | tf_op jit(solution)/shard_map/all_gather | solution.py:38
  991.8 1.4 reshape.54
  993.2 0.2 convert_bitcast_fusion.1
  993.5 3.7 fusion.32
  997.2 0.7 convolution_bitcast_fusion
  997.9 1.3 copy.34
  999.2 0.0 all-reduce.12.cloned.1.call-update
  999.2 0.5 convert_bitcast_fusion
  999.7 4.5 fusion.30
  1004.2 0.3 convolution_bitcast_fusion.4
  1004.5 271.2 %all-reduce.12.cloned.1.call-done = f32[262144]{0:T(1024)} async-done(((f32[262144]{0:T(1024)}), f32[262144]{0:T(1024)}) %all-reduce.12.cloned.1.call-update) | async-done | bytes 1048592
  1275.7 0.8 dynamic-slice_add_fusion
  1276.5 44.3 %psum.60 = f32[8192]{0:T(1024)S(1)} all-reduce(f32[8192]{0:T(1024)S(1)} %dynamic-slice_add_fusion), channel_id=1, replica_groups=mesh['row'=32,'col'=8] {'col'}, use_global_device_ids=true, to_apply=%region_11.12 | all-reduce | flops 8192 | bytes 65536 | tf_op jit(solution)/shard_map/psum | solution.py:55
  1320.8 0.0 copy-done.1
  1320.8 0.6 multiply_reduce_fusion
  1321.4 77.3 %psum.61 = f32[]{:T(128)} all-reduce(f32[]{:T(128)} %get-tuple-element.6), channel_id=1, replica_groups=mesh['row'=32,'col'=8] {'row'}, use_global_device_ids=true, to_apply=%region_13.14 | all-reduce | flops 1 | bytes 8 | tf_op jit(solution)/shard_map/psum | solution.py:57
  1400.0 0.6 broadcast_divide_fusion
  (20 shorter events, 0.3 us)
Async XLA Ops:
  7.2 71.8 %copy-start.2 = (s32[12]{0:T(128)S(1)}, s32[12]{0:T(128)}, u32[]{:S(2)}) copy-start(s32[12]{0:T(128)} %param.7) | copy-start | bytes 148
  7.2 66.4 %all-gather.4.cloned.1.call-start = ((), (), s32[]{:S(2)}) async-start(), calls=%async_computation | async-start | bytes 1081344 | tf_op jit(solution)/shard_map/all_gather | solution.py:38
  8.6 348.9 %all-reduce.8.cloned.1.call-start = ((), (), s32[]{:S(2)}) async-start(), calls=%async_computation.3 | async-start | bytes 2097152
  10.0 71.1 %copy-start.3 = (u32[256]{0:T(256)S(1)}, u32[256]{0:T(256)}, u32[]{:S(2)}) copy-start(u32[256]{0:T(256)} %constant.27) | copy-start | bytes 3076
  78.9 323.6 %copy-start = (s32[8192]{0:T(1024)S(1)}, s32[8192]{0:T(1024)}, u32[]{:S(2)}) copy-start(s32[8192]{0:T(1024)} %param.9) | copy-start | bytes 98308
  81.0 451.7 %all-gather.6.cloned.1.call-start = ((), (), s32[]{:S(2)}) async-start(), calls=%async_computation.1 | async-start | bytes 1081344 | tf_op jit(solution)/shard_map/all_gather | solution.py:38
  482.5 334.2 %all-reduce.10.cloned.1.call-start = ((), (), s32[]{:S(2)}) async-start(), calls=%async_computation.4 | async-start | bytes 2097152
  540.1 451.7 %all-gather.8.cloned.1.call-start = ((), (), s32[]{:S(2)}) async-start(), calls=%async_computation.2 | async-start | bytes 1081344 | tf_op jit(solution)/shard_map/all_gather | solution.py:38
  941.6 334.2 %all-reduce.12.cloned.1.call-start = ((), (), s32[]{:S(2)}) async-start(), calls=%async_computation.5 | async-start | bytes 2097152
  997.2 323.6 %copy-start.1 = (f32[8192]{0:T(1024)S(1)}, f32[8192]{0:T(1024)}, u32[]{:S(2)}) copy-start(f32[8192]{0:T(1024)} %get-tuple-element.8) | copy-start | bytes 98308
Sparse Core Ops, SparseCore 0:
  10.4 63.1 all-gather.3
  81.1 276.3 all-reduce.7
  482.6 50.0 all-gather.5
  540.2 276.3 all-reduce.9
  941.7 50.0 all-gather.7
  999.3 276.3 all-reduce.11
where the time goes:
time: 1410 us
  waiting for transfers between devices  976 us (69%)
  blocking collectives  365 us (26%)
  matrix products  29.5 us (2%)
  between operations  19.5 us (1%)
    unnamed x9, waiting for transfers between devices  812 us
    psum x3, blocking collectives, body(): lax.psum((jnp.sum(bin_sums * mask_float), jnp.sum(mask_float)), 'row')  232 us
    all_gather x3, waiting for transfers between devices, body(): w_full = lax.all_gather(weights, 'row', axis=0, tiled=True)  164 us
    psum x3, blocking collectives, body(): summed = lax.psum(segment_sums, 'col')  133 us
  transfers between devices with their start and end apart: 6, of which 6 were waited for; matrix products, arithmetic and copies ran while one was open for 1% of the time, Pallas kernels for 0%

commit v1 on v0

v1 whole, which is shorter than its diff:
```python
import jax
import jax.numpy as jnp
from jax import lax
from jax.experimental import pallas as pl
from jax.experimental.pallas import tpu as pltpu
from jax.sharding import PartitionSpec as P

IR_MAX = 8
SWEEPS = 3
RB = 16
BS = 512
SLOTS = 12
BAND = SLOTS - IR_MAX
SEL = 64

F32 = jnp.float32
BF16 = jnp.bfloat16
MESH = pl.DeviceIdType.MESH
Z_OFFSETS = (1, 7, 2)
YC_OFFSETS = (4, 3, 5, 2, 6, 1, 7)
X_OFFSETS = (2, 1, 3)


def split2(v):
    hi = v.astype(BF16)
    lo = (v - hi.astype(F32)).astype(BF16)
    return jnp.concatenate([hi, lo], axis=0)


def exact_pick(pick, v):
    out = None
    for _ in range(3):
        term = v.astype(BF16)
        v = v - term.astype(F32)
        part = jnp.dot(pick, term, preferred_element_type=F32)
        out = part if out is None else out + part
    return out


def full_max(v):
    m = jnp.max(jnp.max(v, axis=1, keepdims=True), axis=0, keepdims=True)
    return jnp.where(m > 0, m, 1.0)


def kernel(
    rows_ref, cols_ref, cnt_ref, mask_ref, blocks_ref,
    bias_ref, bal_ref,
    blk, keep, tbuf, ubuf, uloc, ids, pick, pickt,
    tab, selm, rsel, uprev, cparts, pprev, prevp, dense, rz, xp, zh, stz, styc,
    blk_sem, ids_ss, ids_rs, tab_ss, tab_rs, sel_ss, sel_rs, up_ss, up_rs,
    cp_ss, cp_rs, pp_ss, pp_rs, dz_ss, dz_rs, x_ss, x_rs, zh_ss, zh_rs,
    sz_ss, sz_rs, sy_ss, sy_rs,
):
    row = lax.axis_index("row")
    col = lax.axis_index("col")
    zl = row // 8
    yc = lax.rem(row, 8)
    x = col // 2
    z = lax.rem(col, 2) * 4 + zl

    def z_peer(o):
        q = lax.rem(z + o, 8)
        return (lax.rem(q, 4) * 8 + yc, x * 2 + q // 4)

    def yc_peer(o):
        return (zl * 8 + lax.rem(yc + o, 8), col)

    def x_peer(o):
        return (row, lax.rem(x + o, 4) * 2 + lax.rem(col, 2))

    def send(src, dst, ss, rs, dev):
        c = pltpu.make_async_remote_copy(
            src_ref=src, dst_ref=dst, send_sem=ss, recv_sem=rs,
            device_id=dev, device_id_type=MESH,
        )
        c.start()
        return c

    loads = [
        pltpu.make_async_copy(blocks_ref.at[k], blk.at[k], blk_sem.at[k])
        for k in range(SLOTS)
    ]
    for c in loads:
        c.start()

    barrier = pltpu.get_barrier_semaphore()
    peers = (
        [yc_peer(o) for o in range(1, 8)]
        + [z_peer(o) for o in (1, 2, 4, 6, 7)]
        + [x_peer(o) for o in range(1, 4)]
    )
    for dev in peers:
        pl.semaphore_signal(barrier, inc=1, device_id=dev, device_id_type=MESH)

    live = cnt_ref[0]
    row_l = [lax.rem(rows_ref[k], RB) for k in range(SLOTS)]
    col_l = [cols_ref[k] - row * RB for k in range(SLOTS)]
    lane = lax.broadcasted_iota(jnp.int32, (8, 128), 1)
    idv = jnp.zeros((8, 128), jnp.int32)
    for k in range(IR_MAX):
        code = jnp.where(k < live, cols_ref[BAND + k] + 1, 0)
        idv = jnp.where(lane == yc * 8 + k, code, idv)
    ids[yc] = idv
    for q in range(4):
        keep[:, q * 128:(q + 1) * 128] = mask_ref[pl.ds(q, RB, stride=4), :].astype(F32)
    tbuf[0] = jnp.full((RB, BS), 4.0, F32)
    uloc[...] = jnp.zeros_like(uloc)

    pl.semaphore_wait(barrier, len(peers))
    id_copies = [
        send(ids.at[yc], ids.at[yc], ids_ss.at[o - 1], ids_rs.at[o - 1], yc_peer(o))
        for o in YC_OFFSETS
    ]
    for c in loads:
        c.wait()
    for c in id_copies:
        c.wait()
    code = ids[0]
    for p in range(1, 8):
        code = code + ids[p]
    code = code[0:1]
    cc = jnp.maximum(code - 1, 0)
    want = jnp.where(
        (code > 0) & (((cc // 16) % 8) == yc), (cc // 128) * 16 + cc % 16, -1
    )
    full = jnp.where(lax.broadcasted_iota(jnp.int32, (128, 128), 0) == want, 1.0, 0.0)
    pick[...] = full[:SEL, :SEL].astype(BF16)
    pickt[...] = full.T[:SEL, :SEL].astype(BF16)

    iota16 = lax.broadcasted_iota(jnp.int32, (RB, BS), 0)
    iota32 = lax.broadcasted_iota(jnp.int32, (2 * RB, BS), 0)

    def sweep(s, carry):
        u = jnp.where(keep[...] > 0, 4.0 / tbuf[s], 0.0)
        ubuf[s] = u
        own = pl.ds(pl.multiple_of(zl * RB, RB), RB)
        tab[s, own] = u
        c_tab = [
            send(tab.at[s, own], tab.at[s, own], tab_ss.at[s, i], tab_rs.at[s, i], z_peer(o))
            for i, o in enumerate(Z_OFFSETS)
        ]
        uloc[0:RB] = u

        m = full_max(u)
        inv = 1.0 / m
        acc = None
        for k in range(SLOTS):
            if k < BAND:
                target = jnp.where(col_l[k] >= 0, col_l[k], 2 * RB - 8)
            else:
                target = jnp.where(k - BAND < live, RB + k - BAND, -1)
            vec = uloc[pl.ds(row_l[k], 1), :] * inv
            lhs = split2(jnp.where(iota32 == target, vec, 0.0))
            part = jnp.dot(lhs, blk[k], preferred_element_type=F32)
            acc = part if acc is None else acc + part
        acc = (acc[:2 * RB] + acc[2 * RB:]) * m
        band = acc[0:RB]
        cparts[s, yc] = acc[RB:RB + 8]
        pprev[s] = acc[RB + 8:]
        c_cp = [
            send(cparts.at[s, yc], cparts.at[s, yc], cp_ss.at[s, o - 1], cp_rs.at[s, o - 1], yc_peer(o))
            for o in YC_OFFSETS
        ]
        c_pp = send(pprev.at[s], prevp.at[s], pp_ss.at[s], pp_rs.at[s], yc_peer(7))

        for c in c_tab:
            c.wait()
        selm[s] = exact_pick(pickt[...], tab[s])
        c_sel = [
            send(
                selm.at[s, pl.ds(pl.multiple_of(lax.rem(yc + o, 8) * 8, 8), 8)],
                rsel.at[s, yc], sel_ss.at[s, o - 1], sel_rs.at[s, o - 1], yc_peer(o),
            )
            for o in YC_OFFSETS
        ]
        zsel = jnp.where(yc < 7, zl, jnp.maximum(zl - 1, 0))
        c_up = send(
            tab.at[s, pl.ds(pl.multiple_of(zsel * RB + 8, 8), 8)],
            uprev.at[s], up_ss.at[s], up_rs.at[s], yc_peer(1),
        )

        for c in c_cp:
            c.wait()
        c_pp.wait()
        got = jnp.concatenate([cparts[s, p] for p in range(8)], axis=0)
        d = exact_pick(pick[...], got)
        jprev = jnp.where(yc < 7, zl, zl - 1) * RB + RB - 1
        iota64 = lax.broadcasted_iota(jnp.int32, (SEL, BS), 0)
        d = d + jnp.where(iota64 == jprev, prevp[s, 0:1], 0.0)
        dense[s] = d
        c_dz = [
            send(
                dense.at[s, pl.ds(pl.multiple_of(lax.rem(zl + o, 4) * RB, RB), RB)],
                rz.at[s, i], dz_ss.at[s, i], dz_rs.at[s, i], z_peer(o),
            )
            for i, o in enumerate(Z_OFFSETS)
        ]

        for c in c_sel:
            c.wait()
        c_up.wait()
        ucol = selm[s, pl.ds(pl.multiple_of(yc * 8, 8), 8)]
        for o in range(1, 8):
            ucol = ucol + rsel[s, lax.rem(yc + o, 8)]
        uloc[RB:RB + 8] = uprev[s]
        m2 = full_max(jnp.concatenate([uloc[...], ucol], axis=0))
        inv2 = 1.0 / m2
        acc = None
        for k in range(SLOTS):
            if k < BAND:
                vec = uloc[pl.ds(jnp.where((col_l[k] >= 0) & (col_l[k] < RB), col_l[k], RB + 7), 1), :]
                target = row_l[k]
            else:
                vec = ucol[k - BAND:k - BAND + 1]
                target = jnp.where(k - BAND < live, row_l[k], -1)
            lhs = split2(jnp.where(iota16 == target, vec * inv2, 0.0))
            part = lax.dot_general(
                lhs, blk[k], (((1,), (1,)), ((), ())), preferred_element_type=F32
            )
            acc = part if acc is None else acc + part
        total = (acc[:RB] + acc[RB:]) * m2 + band

        for c in c_dz:
            c.wait()
        total = total + dense[s, own] + rz[s, 0] + rz[s, 1] + rz[s, 2]

        xp[s, x] = total
        c_x = [
            send(xp.at[s, x], xp.at[s, x], x_ss.at[s, o - 1], x_rs.at[s, o - 1], x_peer(o))
            for o in X_OFFSETS
        ]
        for c in c_x:
            c.wait()
        zh[s, 0] = (xp[s, 0] + xp[s, 1]) + (xp[s, 2] + xp[s, 3])
        c_zh = send(zh.at[s, 0], zh.at[s, 1], zh_ss.at[s], zh_rs.at[s], z_peer(4))
        c_zh.wait()
        tbuf[s + 1] = zh[s, 0] + zh[s, 1]
        return carry

    lax.fori_loop(0, SWEEPS, sweep, 0)

    kept = keep[...]
    terms = [
        kept,
        tbuf[1] * kept,
        tbuf[2] * ubuf[1],
        tbuf[3] * ubuf[2],
    ]
    sub = lax.broadcasted_iota(jnp.int32, (8, 128), 0)
    stat = jnp.zeros((8, 128), F32)
    for i, v in enumerate(terms):
        v = jnp.sum(jnp.sum(v, axis=1, keepdims=True), axis=0, keepdims=True)
        stat = jnp.where(sub == i, v, stat)
    stz[zl] = stat
    c_sz = [
        send(stz.at[zl], stz.at[zl], sz_ss.at[i], sz_rs.at[i], z_peer(o))
        for i, o in enumerate(Z_OFFSETS)
    ]
    for c in c_sz:
        c.wait()
    styc[yc] = (stz[0] + stz[1]) + (stz[2] + stz[3])
    c_sy = [
        send(styc.at[yc], styc.at[yc], sy_ss.at[o - 1], sy_rs.at[o - 1], yc_peer(o))
        for o in YC_OFFSETS
    ]
    for c in c_sy:
        c.wait()
    stat = styc[0]
    for p in range(1, 8):
        stat = stat + styc[p]
    count = stat[0:1, 0:1]
    mean1 = stat[1:2, 0:1] / count
    mean2 = stat[2:3, 0:1] / count
    mean3 = stat[3:4, 0:1] / count
    scale = mean1 * mean2 * 0.0625 * mean3
    b3 = tbuf[3]
    bias = jnp.where(kept > 0, b3 / scale, 1.0)
    balance = b3 * ubuf[2] / mean3
    for q in range(4):
        bias_ref[pl.ds(q, RB, stride=4), :] = bias[:, q * 128:(q + 1) * 128]
        bal_ref[pl.ds(q, RB, stride=4), :] = balance[:, q * 128:(q + 1) * 128]


def body(blocks, block_rows, block_cols, inter_counts, keep_mask):
    seg = keep_mask.shape[0]
    vm = pl.BlockSpec(memory_space=pltpu.VMEM)
    sm = pl.BlockSpec(memory_space=pltpu.SMEM)
    S = SWEEPS
    dma = pltpu.SemaphoreType.DMA
    out = jax.ShapeDtypeStruct((seg // 128, 128), F32)
    bias, balance = pl.pallas_call(
        kernel,
        out_shape=(out, out),
        in_specs=[sm, sm, sm, vm, pl.BlockSpec(memory_space=pl.ANY)],
        out_specs=(vm, vm),
        scratch_shapes=[
            pltpu.VMEM((SLOTS, BS, BS), BF16),
            pltpu.VMEM((RB, BS), F32),
            pltpu.VMEM((S + 1, RB, BS), F32),
            pltpu.VMEM((S, RB, BS), F32),
            pltpu.VMEM((RB + 8, BS), F32),
            pltpu.VMEM((8, 8, 128), jnp.int32),
            pltpu.VMEM((SEL, SEL), BF16),
            pltpu.VMEM((SEL, SEL), BF16),
            pltpu.VMEM((S, SEL, BS), F32),
            pltpu.VMEM((S, SEL, BS), F32),
            pltpu.VMEM((S, 8, 8, BS), F32),
            pltpu.VMEM((S, 8, BS), F32),
            pltpu.VMEM((S, 8, 8, BS), F32),
            pltpu.VMEM((S, 8, BS), F32),
            pltpu.VMEM((S, 8, BS), F32),
            pltpu.VMEM((S, SEL, BS), F32),
            pltpu.VMEM((S, 3, RB, BS), F32),
            pltpu.VMEM((S, 4, RB, BS), F32),
            pltpu.VMEM((S, 2, RB, BS), F32),
            pltpu.VMEM((4, 8, 128), F32),
            pltpu.VMEM((8, 8, 128), F32),
            dma((SLOTS,)),
            dma((7,)), dma((7,)),
            dma((S, 3)), dma((S, 3)),
            dma((S, 7)), dma((S, 7)),
            dma((S,)), dma((S,)),
            dma((S, 7)), dma((S, 7)),
            dma((S,)), dma((S,)),
            dma((S, 3)), dma((S, 3)),
            dma((S, 3)), dma((S, 3)),
            dma((S,)), dma((S,)),
            dma((3,)), dma((3,)),
            dma((7,)), dma((7,)),
        ],
        compiler_params=pltpu.CompilerParams(
            collective_id=0, has_side_effects=True, vmem_limit_bytes=48 * 2**20
        ),
        name="balance",
    )(block_rows, block_cols, inter_counts, keep_mask.reshape(seg // 128, 128), blocks)
    return bias.reshape(seg), balance.reshape(seg)


def solution(mesh):
    return jax.shard_map(
        body,
        mesh=mesh,
        in_specs=(
            P(("row", "col"), None, None),
            P(("row", "col")),
            P(("row", "col")),
            P(("row", "col")),
            P("row"),
        ),
        out_specs=(P("row"), P("row")),
        check_vma=False,
    )
```

time: 1410 us -> 85.7 us (0.06)
  waiting for transfers between devices: 976 us -> 0 us
  blocking collectives: 365 us -> 0 us
  Pallas kernels: 0 us -> 80.9 us
  matrix products: 29.5 us -> 0 us
  between operations: 19.5 us -> 1.3 us
    unnamed x9 -> x0, waiting for transfers between devices: 812 us -> none
    psum x6 -> x0, blocking collectives: 365 us -> none  [the longest x3 232 us: body(): lax.psum((jnp.sum(bin_sums * mask_float), jnp.sum(mask_float)), 'row')]
    all_gather x3 -> x0, waiting for transfers between devices: 164 us -> none  [body(): w_full = lax.all_gather(weights, 'row', axis=0, tiled=True)]
    pallas_call x0 -> x1, Pallas kernels: none -> 80.9 us  [body(): pl.pallas_call(kernel, out_shape=(out, out), in_specs=[sm, sm, sm, vm, pl...]
    dot_general x18 -> x0, matrix products: 29.5 us -> none  [the longest x3 13.5 us: body(): jnp.einsum('kab,kbt->kat', blocks, pair_cols, preferred_element_type=jnp....]
  transfers between devices with their start and end apart: 6 -> 0, of which waited for: 6 -> 0; matrix products, arithmetic and copies ran while one was open for 1% -> 0% of each run, Pallas kernels for 0% -> 0%
where the time goes in v1:
time: 85.7 us; the launch traced here: 85.5 us
  Pallas kernels  80.9 us (94%)
  local copies, waits for them, and re-layouts  3.3 us (4%)
  between operations  1.3 us (2%)
    pallas_call x1, Pallas kernels, body(): pl.pallas_call(kernel, out_shape=(out, out), in_specs=[sm, sm, sm, vm, pl...  80.9 us
    unnamed x8, local copies, waits for them, and re-layouts  3.3 us

profile of v1, /device:TPU:1, one launch (start us, length us, event | category | flops | bytes accessed | tf_op | source)
XLA Modules:
  0.0 85.5 jit_solution(16880972244778344705)
XLA Ops:
  1.3 0.0 copy-start
  1.3 0.7 copy-done
  2.0 0.0 copy-start.1
  2.0 0.7 copy-done.1
  2.7 0.0 copy-start.2
  2.7 0.7 copy-done.2
  3.3 80.9 %balance.1 = (f32[64,128]{1,0:T(8,128)S(1)}, f32[64,128]{1,0:T(8,128)S(1)}) custom-call(s32[12]{0:T(128)S(1)} %copy-done.1, s32[12]{0:T(128)S(1)} %copy-done.2, s32[1]{0:T(128)S(6)} %copy.9.cnt_ref, s32[64,128]{1,0:T(8,128)S(1)} %bitcast.3, bf16[12,512,512]{2,1,0:T(8,128)(2,1)} %blocks_ref.1), custom_call_target="tpu_custom_call" | custom-call | tf_op jit(solution)/shard_map/balance/pallas_call | solution.py:291
  84.3 0.6 copy.10
  84.9 0.6 copy.11
Async XLA Ops:
  1.3 0.8 copy-start
  2.0 0.7 copy-start.1
  2.7 0.7 copy-start.2

commit v2 on v0

v2 whole, which is shorter than its diff:
```python
import jax
import jax.numpy as jnp
from jax import lax
from jax.experimental import pallas as pl
from jax.experimental.pallas import tpu as pltpu
from jax.sharding import PartitionSpec as P

IR_MAX = 8
SWEEPS = 3
RB = 16
BS = 512
SLOTS = 12
BAND = SLOTS - IR_MAX
SEL = 64

F32 = jnp.float32
BF16 = jnp.bfloat16
MESH = pl.DeviceIdType.MESH
YC_OFFSETS = (4, 5, 3, 2, 6, 1, 7)
X_OFFSETS = ((2, 1), (1, 1), (3, 1), (0, 1), (2, 0), (1, 0), (3, 0))


def split2(v):
    hi = v.astype(BF16)
    lo = (v - hi.astype(F32)).astype(BF16)
    return jnp.concatenate([hi, lo], axis=0)


def exact_pick(pick, v):
    out = None
    for _ in range(3):
        term = v.astype(BF16)
        v = v - term.astype(F32)
        part = jnp.dot(pick, term, preferred_element_type=F32)
        out = part if out is None else out + part
    return out


def full_max(v):
    m = jnp.max(jnp.max(v, axis=1, keepdims=True), axis=0, keepdims=True)
    return jnp.where(m > 0, m, 1.0)


def kernel(
    rows_hbm, cols_hbm, cnt_hbm, mask_hbm, blocks_ref,
    bias_ref, bal_ref,
    rows_ref, cols_ref, cnt_ref, mask_ref,
    blk, keep, tbuf, ubuf, uloc, ids, pick, pickt, stat, rowband, colband,
    tab, selm, rsel, uprev, cparts, pprev, prevp, dense, rz, xp, stz, styc, stx,
    in_sem, blk_sem, ids_ss, ids_rs, tab_ss, tab_rs, sel_ss, sel_rs, up_ss, up_rs,
    cp_ss, cp_rs, pp_ss, pp_rs, dz_ss, dz_rs, x_ss, x_rs,
    sz_ss, sz_rs, sy_ss, sy_rs, sx_ss, sx_rs,
):
    row = lax.axis_index("row")
    col = lax.axis_index("col")
    zl = row // 8
    yc = lax.rem(row, 8)
    x = col // 2
    zh = lax.rem(col, 2)
    z = zh * 4 + zl
    z_offsets = (jnp.where(lax.rem(row, 2) == 0, 2, 6), 1, 7)

    def z_peer(o):
        q = lax.rem(z + o, 8)
        return (lax.rem(q, 4) * 8 + yc, x * 2 + q // 4)

    def yc_peer(o):
        return (zl * 8 + lax.rem(yc + o, 8), col)

    def x_peer(o, h):
        return (row, lax.rem(x + o, 4) * 2 + lax.rem(zh + h, 2))

    def step_peer(o):
        wrap = 7 if o == 1 else 0
        q = jnp.where(yc == wrap, lax.rem(z + o, 8), z)
        return (lax.rem(q, 4) * 8 + lax.rem(yc + o, 8), x * 2 + q // 4)

    def copy(src, dst, ss, rs, dev):
        return pltpu.make_async_remote_copy(
            src_ref=src, dst_ref=dst, send_sem=ss, recv_sem=rs,
            device_id=dev, device_id_type=MESH,
        )

    def seg(i):
        return pl.ds(pl.multiple_of(i * RB, RB), RB)

    def eight(i):
        return pl.ds(pl.multiple_of(i * 8, 8), 8)

    own = seg(zl)

    def tab_copies(s):
        return [
            copy(tab.at[s, own], tab.at[s, own], tab_ss.at[s, i], tab_rs.at[s, i], z_peer(o))
            for i, o in enumerate(z_offsets)
        ]

    def up_copy(s):
        return copy(
            tab.at[s, pl.ds(pl.multiple_of(zl * RB + 8, 8), 8)],
            uprev.at[s], up_ss.at[s], up_rs.at[s], step_peer(1),
        )

    def cp_copies(s):
        return [
            copy(cparts.at[s, eight(yc)], cparts.at[s, eight(yc)],
                 cp_ss.at[s, o - 1], cp_rs.at[s, o - 1], yc_peer(o))
            for o in YC_OFFSETS
        ]

    def pp_copy(s):
        return copy(pprev.at[s], prevp.at[s], pp_ss.at[s], pp_rs.at[s], step_peer(7))

    def sel_copies(s):
        return [
            copy(selm.at[s, eight(lax.rem(yc + o, 8))], rsel.at[s, yc],
                 sel_ss.at[s, o - 1], sel_rs.at[s, o - 1], yc_peer(o))
            for o in YC_OFFSETS
        ]

    def dz_copies(s):
        return [
            copy(dense.at[s, seg(lax.rem(zl + o, 4))], rz.at[s, i],
                 dz_ss.at[s, i], dz_rs.at[s, i], z_peer(o))
            for i, o in enumerate(z_offsets)
        ]

    def x_copies(s):
        return [
            copy(xp.at[s, col], xp.at[s, col], x_ss.at[s, o * 2 + h - 1],
                 x_rs.at[s, o * 2 + h - 1], x_peer(o, h))
            for o, h in X_OFFSETS
        ]

    loads = [
        pltpu.make_async_copy(src, dst, in_sem.at[i])
        for i, (src, dst) in enumerate((
            (rows_hbm, rows_ref), (cols_hbm, cols_ref), (cnt_hbm, cnt_ref), (mask_hbm, mask_ref),
        ))
    ] + [
        pltpu.make_async_copy(blocks_ref.at[k], blk.at[k], blk_sem.at[k])
        for k in (*range(BAND, SLOTS), *range(BAND))
    ]
    for c in loads:
        c.start()

    barrier = pltpu.get_barrier_semaphore()
    peers = (
        [x_peer(o, h) for o in range(1, 4) for h in range(2)]
        + [z_peer(o) for o in range(1, 8)]
        + [yc_peer(o) for o in range(1, 8)]
        + [step_peer(1), step_peer(7)]
    )
    for dev in peers:
        pl.semaphore_signal(barrier, inc=1, device_id=dev, device_id_type=MESH)
    for c in loads[:4]:
        c.wait()

    live = cnt_ref[0]
    row_l = [lax.rem(rows_ref[k], RB) for k in range(SLOTS)]
    col_l = [cols_ref[k] - row * RB for k in range(BAND)]
    here = [(c >= 0) & (c < RB) for c in col_l]
    lane = lax.broadcasted_iota(jnp.int32, (8, 128), 1)
    iota8 = lax.broadcasted_iota(jnp.int32, (8, BS), 0)
    iota16 = lax.broadcasted_iota(jnp.int32, (RB, BS), 0)
    iota24 = lax.broadcasted_iota(jnp.int32, (RB + 8, BS), 0)

    idv = jnp.zeros((8, 128), jnp.int32)
    for k in range(IR_MAX):
        code = jnp.where(k < live, cols_ref[BAND + k] + 1, 0)
        idv = jnp.where(lane == yc * 8 + k, code, idv)
    ids[yc] = idv
    for q in range(4):
        keep[:, q * 128:(q + 1) * 128] = mask_ref[pl.ds(q, RB, stride=4), :].astype(F32)
    tbuf[0] = jnp.full((RB, BS), 4.0, F32)

    def total_of(v):
        return jnp.sum(jnp.sum(v, axis=1, keepdims=True), axis=0, keepdims=True)

    sub = lax.broadcasted_iota(jnp.int32, (8, 128), 0)
    stat[...] = jnp.where(sub == 0, total_of(keep[...]), 0.0)

    def weights(s):
        u = jnp.where(keep[...] > 0, 4.0 / tbuf[s], 0.0)
        ubuf[s] = u
        tab[s, own] = u
        uloc[0:RB] = u

    def inter_columns(s):
        m = full_max(uloc[0:RB])
        inv = 1.0 / m
        acc = None
        for k in range(IR_MAX):
            vec = uloc[pl.ds(row_l[BAND + k], 1), :] * inv
            target = jnp.where(k < live, k, -1)
            lhs = split2(jnp.where(iota8 == target, vec, 0.0))
            part = jnp.dot(lhs, blk[BAND + k], preferred_element_type=F32)
            acc = part if acc is None else acc + part
        cparts[s, eight(yc)] = (acc[:8] + acc[8:]) * m

    def band_columns(s):
        m = full_max(uloc[0:RB])
        inv = 1.0 / m
        acc = None
        for k in range(BAND):
            vec = uloc[pl.ds(row_l[k], 1), :] * inv
            target = jnp.where(here[k], col_l[k], RB)
            lhs = split2(jnp.where(iota24 == target, vec, 0.0))
            part = jnp.dot(lhs, blk[k], preferred_element_type=F32)
            acc = part if acc is None else acc + part
        acc = (acc[:RB + 8] + acc[RB + 8:]) * m
        colband[...] = acc[:RB]
        pprev[s] = acc[RB:]

    weights(0)
    for c in loads[4:4 + IR_MAX]:
        c.wait()
    inter_columns(0)
    for c in loads[4 + IR_MAX:]:
        c.wait()
    band_columns(0)

    pl.semaphore_wait(barrier, len(peers))
    id_copies = [
        copy(ids.at[yc], ids.at[yc], ids_ss.at[o - 1], ids_rs.at[o - 1], yc_peer(o))
        for o in YC_OFFSETS
    ]
    for c in (*tab_copies(0), up_copy(0), *id_copies, *cp_copies(0), pp_copy(0)):
        c.start()

    def sweep(s, carry):
        up_copy(s).wait_recv()
        uloc[RB:RB + 8] = uprev[s]
        m = full_max(uloc[...])
        inv = 1.0 / m
        acc = None
        for k in range(BAND):
            vec = uloc[pl.ds(jnp.where(here[k], col_l[k], RB + 7), 1), :] * inv
            lhs = split2(jnp.where(iota16 == row_l[k], vec, 0.0))
            part = lax.dot_general(
                lhs, blk[k], (((1,), (1,)), ((), ())), preferred_element_type=F32
            )
            acc = part if acc is None else acc + part
        rowband[...] = (acc[:RB] + acc[RB:]) * m

        @pl.when(s == 0)
        def _():
            for c in id_copies:
                c.wait()
            code = ids[0]
            for p in range(1, 8):
                code = code + ids[p]
            code = code[0:1]
            cc = jnp.maximum(code - 1, 0)
            want = jnp.where(
                (code > 0) & (((cc // 16) % 8) == yc), (cc // 128) * 16 + cc % 16, -1
            )
            full = jnp.where(
                lax.broadcasted_iota(jnp.int32, (128, 128), 0) == want, 1.0, 0.0
            )
            pick[...] = full[:SEL, :SEL].astype(BF16)
            pickt[...] = full.T[:SEL, :SEL].astype(BF16)

        for c in tab_copies(s):
            c.wait_recv()
        selm[s] = exact_pick(pickt[...], tab[s])
        for c in sel_copies(s):
            c.start()

        for c in cp_copies(s):
            c.wait_recv()
        dense[s] = exact_pick(pick[...], cparts[s])
        for c in dz_copies(s):
            c.start()

        share = total_of(dense[s] * tab[s]) + total_of(uloc[0:RB] * rowband[...])
        stat[...] = jnp.where(sub == s + 1, share, stat[...])

        @pl.when(s == SWEEPS - 1)
        def _():
            stz[z] = stat[...]
            for o in range(1, 8):
                copy(stz.at[z], stz.at[z], sz_ss.at[o - 1], sz_rs.at[o - 1], z_peer(o)).start()

        for c in sel_copies(s):
            c.wait_recv()
        ucol = selm[s, eight(yc)]
        for o in range(1, 8):
            ucol = ucol + rsel[s, lax.rem(yc + o, 8)]
        m2 = full_max(ucol)
        ucol = ucol * (1.0 / m2)
        acc = None
        for k in range(IR_MAX):
            target = jnp.where(k < live, row_l[BAND + k], -1)
            lhs = split2(jnp.where(iota16 == target, ucol[k:k + 1], 0.0))
            part = lax.dot_general(
                lhs, blk[BAND + k], (((1,), (1,)), ((), ())), preferred_element_type=F32
            )
            acc = part if acc is None else acc + part
        total = (acc[:RB] + acc[RB:]) * m2 + rowband[...] + colband[...] + dense[s, own]

        pp_copy(s).wait_recv()
        total = total + jnp.where(iota16 == RB - 1, prevp[s, 0:1], 0.0)
        for c in dz_copies(s):
            c.wait_recv()
        total = total + rz[s, 0] + rz[s, 1] + rz[s, 2]

        xp[s, col] = total
        for c in x_copies(s):
            c.start()

        @pl.when(s == SWEEPS - 1)
        def _():
            for o in range(1, 8):
                copy(stz.at[z], stz.at[z], sz_ss.at[o - 1], sz_rs.at[o - 1], z_peer(o)).wait()
            v = stz[0]
            for p in range(1, 8):
                v = v + stz[p]
            styc[yc] = v
            c_sy = [
                copy(styc.at[yc], styc.at[yc], sy_ss.at[o - 1], sy_rs.at[o - 1], yc_peer(o))
                for o in YC_OFFSETS
            ]
            for c in c_sy:
                c.start()
            for c in c_sy:
                c.wait()
            v = styc[0]
            for p in range(1, 8):
                v = v + styc[p]
            stx[x] = v
            for o in range(1, 4):
                copy(stx.at[x], stx.at[x], sx_ss.at[o - 1], sx_rs.at[o - 1], x_peer(o, 0)).start()

        for c in (*tab_copies(s), up_copy(s), *cp_copies(s), pp_copy(s),
                  *sel_copies(s), *dz_copies(s)):
            c.wait_send()
        for c in x_copies(s):
            c.wait()
        t = xp[s, 0]
        for p in range(1, 8):
            t = t + xp[s, p]
        tbuf[s + 1] = t

        @pl.when(s < SWEEPS - 1)
        def _():
            n = s + 1
            weights(n)
            for c in (*tab_copies(n), up_copy(n)):
                c.start()
            inter_columns(n)
            for c in cp_copies(n):
                c.start()
            band_columns(n)
            pp_copy(n).start()

        return carry

    lax.fori_loop(0, SWEEPS, sweep, 0)

    for o in range(1, 4):
        copy(stx.at[x], stx.at[x], sx_ss.at[o - 1], sx_rs.at[o - 1], x_peer(o, 0)).wait()
    v = (stx[0] + stx[1]) + (stx[2] + stx[3])
    count = v[0:1, 0:1] * 0.125
    mean1 = v[1:2, 0:1] * 2.0 / count
    mean2 = v[2:3, 0:1] * 2.0 / count
    mean3 = v[3:4, 0:1] * 2.0 / count
    scale = mean1 * mean2 * 0.0625 * mean3
    b3 = tbuf[SWEEPS]
    bias = jnp.where(keep[...] > 0, b3 / scale, 1.0)
    balance = b3 * ubuf[SWEEPS - 1] / mean3
    for q in range(4):
        bias_ref[pl.ds(q, RB, stride=4), :] = bias[:, q * 128:(q + 1) * 128]
        bal_ref[pl.ds(q, RB, stride=4), :] = balance[:, q * 128:(q + 1) * 128]


def body(blocks, block_rows, block_cols, inter_counts, keep_mask):
    seg = keep_mask.shape[0]
    vm = pl.BlockSpec(memory_space=pltpu.VMEM)
    hbm = pl.BlockSpec(memory_space=pl.ANY)
    S = SWEEPS
    dma = pltpu.SemaphoreType.DMA
    i32 = jnp.int32
    out = jax.ShapeDtypeStruct((seg // 128, 128), F32)
    bias, balance = pl.pallas_call(
        kernel,
        out_shape=(out, out),
        in_specs=[hbm] * 5,
        out_specs=(vm, vm),
        scratch_shapes=[
            pltpu.SMEM((SLOTS,), i32),
            pltpu.SMEM((SLOTS,), i32),
            pltpu.SMEM((1,), i32),
            pltpu.VMEM((seg // 128, 128), i32),
            pltpu.VMEM((SLOTS, BS, BS), BF16),
            pltpu.VMEM((RB, BS), F32),
            pltpu.VMEM((S + 1, RB, BS), F32),
            pltpu.VMEM((S, RB, BS), F32),
            pltpu.VMEM((RB + 8, BS), F32),
            pltpu.VMEM((8, 8, 128), i32),
            pltpu.VMEM((SEL, SEL), BF16),
            pltpu.VMEM((SEL, SEL), BF16),
            pltpu.VMEM((8, 128), F32),
            pltpu.VMEM((RB, BS), F32),
            pltpu.VMEM((RB, BS), F32),
            pltpu.VMEM((S, SEL, BS), F32),
            pltpu.VMEM((S, SEL, BS), F32),
            pltpu.VMEM((S, 8, 8, BS), F32),
            pltpu.VMEM((S, 8, BS), F32),
            pltpu.VMEM((S, SEL, BS), F32),
            pltpu.VMEM((S, 8, BS), F32),
            pltpu.VMEM((S, 8, BS), F32),
            pltpu.VMEM((S, SEL, BS), F32),
            pltpu.VMEM((S, 3, RB, BS), F32),
            pltpu.VMEM((S, 8, RB, BS), F32),
            pltpu.VMEM((8, 8, 128), F32),
            pltpu.VMEM((8, 8, 128), F32),
            pltpu.VMEM((4, 8, 128), F32),
            dma((4,)),
            dma((SLOTS,)),
            dma((7,)), dma((7,)),
            dma((S, 3)), dma((S, 3)),
            dma((S, 7)), dma((S, 7)),
            dma((S,)), dma((S,)),
            dma((S, 7)), dma((S, 7)),
            dma((S,)), dma((S,)),
            dma((S, 3)), dma((S, 3)),
            dma((S, 7)), dma((S, 7)),
            dma((7,)), dma((7,)),
            dma((7,)), dma((7,)),
            dma((3,)), dma((3,)),
        ],
        compiler_params=pltpu.CompilerParams(
            collective_id=0, has_side_effects=True, vmem_limit_bytes=48 * 2**20
        ),
        name="balance",
    )(block_rows, block_cols, inter_counts, keep_mask.reshape(seg // 128, 128), blocks)
    return bias.reshape(seg), balance.reshape(seg)


def solution(mesh):
    return jax.shard_map(
        body,
        mesh=mesh,
        in_specs=(
            P(("row", "col"), None, None),
            P(("row", "col")),
            P(("row", "col")),
            P(("row", "col")),
            P("row"),
        ),
        out_specs=(P("row"), P("row")),
        check_vma=False,
    )
```

time: 1410 us -> 74.3 us (0.05)
  waiting for transfers between devices: 976 us -> 0 us
  blocking collectives: 365 us -> 0 us
  Pallas kernels: 0 us -> 69.3 us
  matrix products: 29.5 us -> 0 us
  between operations: 19.5 us -> 1.3 us
    unnamed x9 -> x0, waiting for transfers between devices: 812 us -> none
    psum x6 -> x0, blocking collectives: 365 us -> none  [the longest x3 232 us: body(): lax.psum((jnp.sum(bin_sums * mask_float), jnp.sum(mask_float)), 'row')]
    all_gather x3 -> x0, waiting for transfers between devices: 164 us -> none  [body(): w_full = lax.all_gather(weights, 'row', axis=0, tiled=True)]
    pallas_call x0 -> x1, Pallas kernels: none -> 69.3 us  [body(): pl.pallas_call(kernel, out_shape=(out, out), in_specs=[hbm] * 5, out_spec...]
    dot_general x18 -> x0, matrix products: 29.5 us -> none  [the longest x3 13.5 us: body(): jnp.einsum('kab,kbt->kat', blocks, pair_cols, preferred_element_type=jnp....]
  transfers between devices with their start and end apart: 6 -> 0, of which waited for: 6 -> 0; matrix products, arithmetic and copies ran while one was open for 1% -> 0% of each run, Pallas kernels for 0% -> 0%
where the time goes in v2:
time: 74.3 us; the launch traced here: 73.9 us
  Pallas kernels  69.3 us (93%)
  local copies, waits for them, and re-layouts  3.3 us (4%)
  between operations  1.3 us (2%)
    pallas_call x1, Pallas kernels, body(): pl.pallas_call(kernel, out_shape=(out, out), in_specs=[hbm] * 5, out_spec...  69.3 us
    unnamed x8, local copies, waits for them, and re-layouts  3.3 us

profile of v2, /device:TPU:1, one launch (start us, length us, event | category | flops | bytes accessed | tf_op | source)
XLA Modules:
  0.0 73.9 jit_solution(9200747944535340488)
XLA Ops:
  1.3 0.0 copy-start
  1.3 0.7 %copy-done = s32[8192]{0:T(1024)S(1)} copy-done((s32[8192]{0:T(1024)S(1)}, s32[8192]{0:T(1024)}, u32[]{:S(2)}) %copy-start) | copy-done | bytes 32792
  2.0 0.0 copy-start.1
  2.0 0.7 copy-done.1
  2.7 0.0 copy-start.2
  2.7 0.7 copy-done.2
  3.3 69.3 %balance.1 = (f32[64,128]{1,0:T(8,128)S(1)}, f32[64,128]{1,0:T(8,128)S(1)}) custom-call(s32[12]{0:T(128)S(1)} %copy-done.1, s32[12]{0:T(128)S(1)} %copy-done.2, s32[1]{0:T(128)S(6)} %copy.9.cnt_hbm, s32[64,128]{1,0:T(8,128)S(1)} %bitcast.3, bf16[12,512,512]{2,1,0:T(8,128)(2,1)} %blocks_ref.1), custom_call_target="tpu_custom_call" | custom-call | tf_op jit(solution)/shard_map/balance/pallas_call | solution.py:385
  72.7 0.6 copy.10
  73.3 0.6 copy.11
Async XLA Ops:
  1.3 0.8 %copy-start = (s32[8192]{0:T(1024)S(1)}, s32[8192]{0:T(1024)}, u32[]{:S(2)}) copy-start(s32[8192]{0:T(1024)} %param.9) | copy-start | bytes 98308
  2.0 0.7 copy-start.1
  2.7 0.7 copy-start.2

commit v3 on v2

--- a/solution.py
+++ b/solution.py
@@ -17,7 +17,7 @@
 BF16 = jnp.bfloat16
 MESH = pl.DeviceIdType.MESH
 YC_OFFSETS = (4, 5, 3, 2, 6, 1, 7)
-X_OFFSETS = ((2, 1), (1, 1), (3, 1), (0, 1), (2, 0), (1, 0), (3, 0))
+X_OFFSETS = (2, 1, 3)
 
 
 def split2(v):
@@ -46,9 +46,9 @@
     bias_ref, bal_ref,
     rows_ref, cols_ref, cnt_ref, mask_ref,
     blk, keep, tbuf, ubuf, uloc, ids, pick, pickt, stat, rowband, colband,
-    tab, selm, rsel, uprev, cparts, pprev, prevp, dense, rz, xp, stz, styc, stx,
+    tab, selm, rsel, ulast, uprev, cparts, pprev, prevp, dense, rz, xp, zp, stz, styc, stx,
     in_sem, blk_sem, ids_ss, ids_rs, tab_ss, tab_rs, sel_ss, sel_rs, up_ss, up_rs,
-    cp_ss, cp_rs, pp_ss, pp_rs, dz_ss, dz_rs, x_ss, x_rs,
+    cp_ss, cp_rs, pp_ss, pp_rs, dz_ss, dz_rs, x_ss, x_rs, zh_ss, zh_rs,
     sz_ss, sz_rs, sy_ss, sy_rs, sx_ss, sx_rs,
 ):
     row = lax.axis_index("row")
@@ -67,8 +67,8 @@
     def yc_peer(o):
         return (zl * 8 + lax.rem(yc + o, 8), col)
 
-    def x_peer(o, h):
-        return (row, lax.rem(x + o, 4) * 2 + lax.rem(zh + h, 2))
+    def x_peer(o):
+        return (row, lax.rem(x + o, 4) * 2 + zh)
 
     def step_peer(o):
         wrap = 7 if o == 1 else 0
@@ -97,8 +97,7 @@
 
     def up_copy(s):
         return copy(
-            tab.at[s, pl.ds(pl.multiple_of(zl * RB + 8, 8), 8)],
-            uprev.at[s], up_ss.at[s], up_rs.at[s], step_peer(1),
+            ulast.at[s], uprev.at[s], up_ss.at[s], up_rs.at[s], step_peer(1),
         )
 
     def cp_copies(s):
@@ -125,12 +124,18 @@
             for i, o in enumerate(z_offsets)
         ]
 
-    def x_copies(s):
+    def x_copies(s, h):
         return [
-            copy(xp.at[s, col], xp.at[s, col], x_ss.at[s, o * 2 + h - 1],
-                 x_rs.at[s, o * 2 + h - 1], x_peer(o, h))
-            for o, h in X_OFFSETS
+            copy(xp.at[s, h, x], xp.at[s, h, x], x_ss.at[s, h, o - 1],
+                 x_rs.at[s, h, o - 1], x_peer(o))
+            for o in X_OFFSETS
         ]
+
+    def zh_copy(s, h):
+        return copy(zp.at[s, h, 0], zp.at[s, h, 1], zh_ss.at[s, h], zh_rs.at[s, h], z_peer(4))
+
+    def x_sum(s, h):
+        return (xp[s, h, 0] + xp[s, h, 1]) + (xp[s, h, 2] + xp[s, h, 3])
 
     loads = [
         pltpu.make_async_copy(src, dst, in_sem.at[i])
@@ -146,7 +151,7 @@
 
     barrier = pltpu.get_barrier_semaphore()
     peers = (
-        [x_peer(o, h) for o in range(1, 4) for h in range(2)]
+        [x_peer(o) for o in range(1, 4)]
         + [z_peer(o) for o in range(1, 8)]
         + [yc_peer(o) for o in range(1, 8)]
         + [step_peer(1), step_peer(7)]
@@ -173,6 +178,7 @@
     for q in range(4):
         keep[:, q * 128:(q + 1) * 128] = mask_ref[pl.ds(q, RB, stride=4), :].astype(F32)
     tbuf[0] = jnp.full((RB, BS), 4.0, F32)
+    uloc[...] = jnp.zeros_like(uloc)
 
     def total_of(v):
         return jnp.sum(jnp.sum(v, axis=1, keepdims=True), axis=0, keepdims=True)
@@ -185,6 +191,7 @@
         ubuf[s] = u
         tab[s, own] = u
         uloc[0:RB] = u
+        ulast[s] = u[RB - 1:]
 
     def inter_columns(s):
         m = full_max(uloc[0:RB])
@@ -210,32 +217,51 @@
             acc = part if acc is None else acc + part
         acc = (acc[:RB + 8] + acc[RB + 8:]) * m
         colband[...] = acc[:RB]
-        pprev[s] = acc[RB:]
-
+        pprev[s] = acc[RB:RB + 1]
+
+    def add_share(s):
+        share = total_of(dense[s] * tab[s]) + total_of(uloc[0:RB] * rowband[...])
+        stat[...] = jnp.where(sub == s + 1, share, stat[...])
+
+    def first_columns():
+        for c in loads[4:4 + IR_MAX]:
+            c.wait()
+        inter_columns(0)
+
+    early = z < 4
     weights(0)
-    for c in loads[4:4 + IR_MAX]:
-        c.wait()
-    inter_columns(0)
-    for c in loads[4 + IR_MAX:]:
-        c.wait()
-    band_columns(0)
+
+    @pl.when(early)
+    def _():
+        first_columns()
 
     pl.semaphore_wait(barrier, len(peers))
     id_copies = [
         copy(ids.at[yc], ids.at[yc], ids_ss.at[o - 1], ids_rs.at[o - 1], yc_peer(o))
         for o in YC_OFFSETS
     ]
-    for c in (*tab_copies(0), up_copy(0), *id_copies, *cp_copies(0), pp_copy(0)):
+    for c in (*tab_copies(0), up_copy(0), *id_copies):
         c.start()
+
+    @pl.when(jnp.logical_not(early))
+    def _():
+        first_columns()
+
+    for c in cp_copies(0):
+        c.start()
+    for c in loads[4 + IR_MAX:]:
+        c.wait()
+    band_columns(0)
+    pp_copy(0).start()
 
     def sweep(s, carry):
         up_copy(s).wait_recv()
-        uloc[RB:RB + 8] = uprev[s]
+        uloc[RB:RB + 1] = uprev[s]
         m = full_max(uloc[...])
         inv = 1.0 / m
         acc = None
         for k in range(BAND):
-            vec = uloc[pl.ds(jnp.where(here[k], col_l[k], RB + 7), 1), :] * inv
+            vec = uloc[pl.ds(jnp.where(here[k], col_l[k], RB), 1), :] * inv
             lhs = split2(jnp.where(iota16 == row_l[k], vec, 0.0))
             part = lax.dot_general(
                 lhs, blk[k], (((1,), (1,)), ((), ())), preferred_element_type=F32
@@ -273,11 +299,9 @@
         for c in dz_copies(s):
             c.start()
 
-        share = total_of(dense[s] * tab[s]) + total_of(uloc[0:RB] * rowband[...])
-        stat[...] = jnp.where(sub == s + 1, share, stat[...])
-
         @pl.when(s == SWEEPS - 1)
         def _():
+            add_share(s)
             stz[z] = stat[...]
             for o in range(1, 8):
                 copy(stz.at[z], stz.at[z], sz_ss.at[o - 1], sz_rs.at[o - 1], z_peer(o)).start()
@@ -300,13 +324,33 @@
         total = (acc[:RB] + acc[RB:]) * m2 + rowband[...] + colband[...] + dense[s, own]
 
         pp_copy(s).wait_recv()
-        total = total + jnp.where(iota16 == RB - 1, prevp[s, 0:1], 0.0)
+        total = total + jnp.where(iota16 == RB - 1, prevp[s], 0.0)
         for c in dz_copies(s):
             c.wait_recv()
         total = total + rz[s, 0] + rz[s, 1] + rz[s, 2]
 
-        xp[s, col] = total
-        for c in x_copies(s):
+        half = BS // 2
+        zp[s, 1, 0] = total[:, half:]
+        zh_copy(s, 1).start()
+        xp[s, 0, x] = total[:, :half]
+        for c in x_copies(s, 0):
+            c.start()
+
+        @pl.when(s < SWEEPS - 1)
+        def _():
+            add_share(s)
+
+        for c in (*tab_copies(s), up_copy(s), *cp_copies(s), pp_copy(s),
+                  *sel_copies(s), *dz_copies(s)):
+            c.wait_send()
+
+        for c in x_copies(s, 0):
+            c.wait_recv()
+        zp[s, 0, 0] = x_sum(s, 0)
+        zh_copy(s, 0).start()
+        zh_copy(s, 1).wait_recv()
+        xp[s, 1, x] = zp[s, 1, 0] + zp[s, 1, 1]
+        for c in x_copies(s, 1):
             c.start()
 
         @pl.when(s == SWEEPS - 1)
@@ -330,17 +374,16 @@
                 v = v + styc[p]
             stx[x] = v
             for o in range(1, 4):
-                copy(stx.at[x], stx.at[x], sx_ss.at[o - 1], sx_rs.at[o - 1], x_peer(o, 0)).start()
-
-        for c in (*tab_copies(s), up_copy(s), *cp_copies(s), pp_copy(s),
-                  *sel_copies(s), *dz_copies(s)):
-            c.wait_send()
-        for c in x_copies(s):
-            c.wait()
-        t = xp[s, 0]
-        for p in range(1, 8):
-            t = t + xp[s, p]
-        tbuf[s + 1] = t
+                copy(stx.at[x], stx.at[x], sx_ss.at[o - 1], sx_rs.at[o - 1], x_peer(o)).start()
+
+        for h in range(2):
+            for c in (zh_copy(s, h), *x_copies(s, h)):
+                c.wait_send()
+        for c in x_copies(s, 1):
+            c.wait_recv()
+        tbuf[s + 1, :, half:] = x_sum(s, 1)
+        zh_copy(s, 0).wait_recv()
+        tbuf[s + 1, :, :half] = zp[s, 0, 0] + zp[s, 0, 1]
 
         @pl.when(s < SWEEPS - 1)
         def _():
@@ -359,7 +402,7 @@
     lax.fori_loop(0, SWEEPS, sweep, 0)
 
     for o in range(1, 4):
-        copy(stx.at[x], stx.at[x], sx_ss.at[o - 1], sx_rs.at[o - 1], x_peer(o, 0)).wait()
+        copy(stx.at[x], stx.at[x], sx_ss.at[o - 1], sx_rs.at[o - 1], x_peer(o)).wait()
     v = (stx[0] + stx[1]) + (stx[2] + stx[3])
     count = v[0:1, 0:1] * 0.125
     mean1 = v[1:2, 0:1] * 2.0 / count
@@ -377,7 +420,7 @@
 def body(blocks, block_rows, block_cols, inter_counts, keep_mask):
     seg = keep_mask.shape[0]
     vm = pl.BlockSpec(memory_space=pltpu.VMEM)
-    hbm = pl.BlockSpec(memory_space=pl.ANY)
+    hbm = pl.BlockSpec(memory_space=pltpu.HBM)
     S = SWEEPS
     dma = pltpu.SemaphoreType.DMA
     i32 = jnp.int32
@@ -406,13 +449,15 @@
             pltpu.VMEM((S, SEL, BS), F32),
             pltpu.VMEM((S, SEL, BS), F32),
             pltpu.VMEM((S, 8, 8, BS), F32),
-            pltpu.VMEM((S, 8, BS), F32),
+            pltpu.VMEM((S, 1, BS), F32),
+            pltpu.VMEM((S, 1, BS), F32),
             pltpu.VMEM((S, SEL, BS), F32),
-            pltpu.VMEM((S, 8, BS), F32),
-            pltpu.VMEM((S, 8, BS), F32),
+            pltpu.VMEM((S, 1, BS), F32),
+            pltpu.VMEM((S, 1, BS), F32),
             pltpu.VMEM((S, SEL, BS), F32),
             pltpu.VMEM((S, 3, RB, BS), F32),
-            pltpu.VMEM((S, 8, RB, BS), F32),
+            pltpu.VMEM((S, 2, 4, RB, BS // 2), F32),
+            pltpu.VMEM((S, 2, 2, RB, BS // 2), F32),
             pltpu.VMEM((8, 8, 128), F32),
             pltpu.VMEM((8, 8, 128), F32),
             pltpu.VMEM((4, 8, 128), F32),
@@ -425,13 +470,14 @@
             dma((S, 7)), dma((S, 7)),
             dma((S,)), dma((S,)),
             dma((S, 3)), dma((S, 3)),
-            dma((S, 7)), dma((S, 7)),
+            dma((S, 2, 3)), dma((S, 2, 3)),
+            dma((S, 2)), dma((S, 2)),
             dma((7,)), dma((7,)),
             dma((7,)), dma((7,)),
             dma((3,)), dma((3,)),
         ],
         compiler_params=pltpu.CompilerParams(
-            collective_id=0, has_side_effects=True, vmem_limit_bytes=48 * 2**20
+            collective_id=0, has_side_effects=True, vmem_limit_bytes=58 * 2**20
         ),
         name="balance",
     )(block_rows, block_cols, inter_counts, keep_mask.reshape(seg // 128, 128), blocks)

time: 74.3 us -> 73.2 us (0.985)
    unnamed x8 -> x2, local copies, waits for them, and re-layouts: 3.3 us -> 2.75 us
where the time goes in v3:
time: 73.2 us; the launch traced here: 72.9 us
  Pallas kernels  68.9 us (94%)
  local copies, waits for them, and re-layouts  2.75 us (4%)
  between operations  1.29 us (2%)
    pallas_call x1, Pallas kernels, body(): pl.pallas_call(kernel, out_shape=(out, out), in_specs=[hbm] * 5, out_spec...  68.9 us
    unnamed x2, local copies, waits for them, and re-layouts  2.75 us

profile of v3, /device:TPU:1, one launch (start us, length us, event | category | flops | bytes accessed | tf_op | source)
XLA Modules:
  0.0 72.9 jit_solution(13742790259677811885)
XLA Ops:
  1.3 68.9 %balance.1 = (f32[64,128]{1,0:T(8,128)}, f32[64,128]{1,0:T(8,128)}) custom-call(s32[12]{0:T(128)} %rows_hbm.1, s32[12]{0:T(128)} %cols_hbm.1, s32[1]{0:T(128)S(6)} %copy.9.cnt_hbm, s32[64,128]{1,0:T(8,128)} %bitcast.3, bf16[12,512,512]{2,1,0:T(8,128)(2,1)} %blocks_ref.1), custom_call_target="tpu_custom_call" | custom-call | tf_op jit(solution)/shard_map/balance/pallas_call | solution.py:428
  70.2 1.4 %copy.10 = f32[8192]{0:T(1024)} copy(f32[8192]{0:T(1024)} %bitcast.5) | data formatting | bytes 65536
  71.6 1.4 %copy.11 = f32[8192]{0:T(1024)} copy(f32[8192]{0:T(1024)} %bitcast.4) | data formatting | bytes 65536

commit v4 on v2

v4 whole, which is shorter than its diff:
```python
import jax
import jax.numpy as jnp
from jax import lax
from jax.experimental import pallas as pl
from jax.experimental.pallas import tpu as pltpu
from jax.sharding import PartitionSpec as P

IR_MAX = 8
SWEEPS = 3
RB = 16
BS = 512
SLOTS = 12
BAND = SLOTS - IR_MAX
SEL = 64
VMEM_LIMIT = 58 * 2**20

F32 = jnp.float32
BF16 = jnp.bfloat16
MESH = pl.DeviceIdType.MESH
RING = (2, 1, 3)


def split2(v):
    hi = v.astype(BF16)
    lo = (v - hi.astype(F32)).astype(BF16)
    return jnp.concatenate([hi, lo], axis=0)


def exact_pick(pick, v):
    out = None
    for _ in range(3):
        term = v.astype(BF16)
        v = v - term.astype(F32)
        part = jnp.dot(pick, term, preferred_element_type=F32)
        out = part if out is None else out + part
    return out


def full_max(v):
    m = jnp.max(jnp.max(v, axis=1, keepdims=True), axis=0, keepdims=True)
    return jnp.where(m > 0, m, 1.0)


def kernel(
    rows_hbm, cols_hbm, cnt_hbm, mask_hbm, blocks_ref,
    bias_ref, bal_ref,
    rows_ref, cols_ref, cnt_ref, mask_ref,
    blk, keep, tbuf, ubuf, uloc, ids, pick, pickt, stat, rowband, colband,
    tab, selm, rsel, ulast, uprev, cparts, pprev, prevp, dense, rz,
    xa, za, ta, zb, xb, tb, wstat, stz, sty, stx, fin,
    in_sem, blk_sem, ids_ss, ids_rs, tab_ss, tab_rs, sel_ss, sel_rs, up_ss, up_rs,
    cp_ss, cp_rs, pp_ss, pp_rs, dz_ss, dz_rs, xa_ss, xa_rs, za_ss, za_rs,
    zb_ss, zb_rs, xb_ss, xb_rs, ws_ss, ws_rs,
    sz_ss, sz_rs, sy_ss, sy_rs, sx_ss, sx_rs, fin_ss, fin_rs,
):
    row = lax.axis_index("row")
    col = lax.axis_index("col")
    zl = row // 8
    yc = lax.rem(row, 8)
    y = yc // 2
    core = lax.rem(row, 2)
    x = col // 2
    zh = lax.rem(col, 2)
    z = zh * 4 + zl
    half = BS // 2
    hub = core == 1
    worker = core == 0
    inner = jnp.where(zl < 2, 2, 6)
    two = (inner, 8 - inner)

    def chip(xx, yy, zz, cc):
        return (lax.rem(zz, 4) * 8 + yy * 2 + cc, xx * 2 + zz // 4)

    def z_peer(o, c):
        return chip(x, y, lax.rem(z + o, 8), c)

    def y_peer(o, c):
        return chip(x, lax.rem(y + o, 4), z, c)

    def x_peer(o, c):
        return chip(lax.rem(x + o, 4), y, z, c)

    def sibling(c):
        return chip(x, y, z, c)

    def step_peer(o):
        wrap = 7 if o == 1 else 0
        q = jnp.where(yc == wrap, lax.rem(z + o, 8), z)
        return (lax.rem(q, 4) * 8 + lax.rem(yc + o, 8), x * 2 + q // 4)

    def copy(src, dst, ss, rs, dev):
        return pltpu.make_async_remote_copy(
            src_ref=src, dst_ref=dst, send_sem=ss, recv_sem=rs,
            device_id=dev, device_id_type=MESH,
        )

    def seg(q, c):
        return pl.ds(pl.multiple_of(q * 2 * RB + c * RB, RB), RB)

    def eight(i):
        return pl.ds(pl.multiple_of(i * 8, 8), 8)

    own = seg(zl, core)
    mine = eight(yc)

    def tab_copies(s, c):
        out = [
            copy(tab.at[s, own], tab.at[s, own], tab_ss.at[s, i], tab_rs.at[s, i, c], z_peer(o, 1))
            for i, o in enumerate((two[c], 1, 7))
        ]
        if c == 0:
            out.append(copy(tab.at[s, own], tab.at[s, own], tab_ss.at[s, 3], tab_rs.at[s, 3, 0], sibling(1)))
        return out

    def ids_copies(c):
        out = [copy(ids.at[yc], ids.at[yc], ids_ss.at[o - 1], ids_rs.at[o - 1, c], y_peer(o, 1)) for o in RING]
        if c == 0:
            out.append(copy(ids.at[yc], ids.at[yc], ids_ss.at[3], ids_rs.at[3, 0], sibling(1)))
        return out

    def cp_copies(s, c):
        out = [
            copy(cparts.at[s, mine], cparts.at[s, mine], cp_ss.at[s, o - 1], cp_rs.at[s, o - 1, c], y_peer(o, 1))
            for o in RING
        ]
        if c == 0:
            out.append(copy(cparts.at[s, mine], cparts.at[s, mine], cp_ss.at[s, 3], cp_rs.at[s, 3, 0], sibling(1)))
        return out

    def up_copy(s):
        return copy(ulast.at[s], uprev.at[s], up_ss.at[s], up_rs.at[s], step_peer(1))

    def pp_copy(s):
        return copy(pprev.at[s], prevp.at[s], pp_ss.at[s], pp_rs.at[s], step_peer(7))

    def sel_copies(s):
        out = [
            copy(selm.at[s, eight(lax.rem(y + o, 4) * 2 + c)], rsel.at[s, y],
                 sel_ss.at[s, o - 1, c], sel_rs.at[s, o - 1], y_peer(o, c))
            for o in RING for c in (0, 1)
        ]
        return out + [copy(selm.at[s, eight(y * 2)], rsel.at[s, y], sel_ss.at[s, 3, 0], sel_rs.at[s, 3], sibling(0))]

    def dz_copies(s):
        out = [
            copy(dense.at[s, seg(lax.rem(zl + o, 4), c)], rz.at[s, i],
                 dz_ss.at[s, i, c], dz_rs.at[s, i], z_peer(o, c))
            for c in (0, 1) for i, o in enumerate((two[c], 1, 7))
        ]
        return out + [copy(dense.at[s, seg(zl, 0)], rz.at[s, 3], dz_ss.at[s, 3, 0], dz_rs.at[s, 3], sibling(0))]

    def xa_copies(s, c):
        out = [
            copy(xa.at[s, c, x], xa.at[s, c, x], xa_ss.at[s, o - 1], xa_rs.at[s, o - 1, c], x_peer(o, 1))
            for o in RING
        ]
        if c == 0:
            out.append(copy(xa.at[s, 0, x], xa.at[s, 0, x], xa_ss.at[s, 3], xa_rs.at[s, 3, 0], sibling(1)))
        return out

    def za_copies(s):
        return [
            copy(za.at[s], ta.at[s, 1], za_ss.at[s, 0], za_rs.at[s, 1], z_peer(4, 0)),
            copy(ta.at[s, 0], ta.at[s, 1], za_ss.at[s, 1], za_rs.at[s, 1], z_peer(4, 1)),
            copy(za.at[s], ta.at[s, 0], za_ss.at[s, 2], za_rs.at[s, 0], sibling(0)),
        ]

    def zb_copies(s, c):
        out = [copy(zb.at[s, c, 0], zb.at[s, c, 1], zb_ss.at[s, 0], zb_rs.at[s, 0, c], z_peer(4, 1))]
        if c == 0:
            out.append(copy(zb.at[s, 0, 0], zb.at[s, 0, 0], zb_ss.at[s, 1], zb_rs.at[s, 1, 0], sibling(1)))
        return out

    def xb_copies(s):
        out = []
        for o in RING:
            out.append(copy(xb.at[s], tb.at[s, x], xb_ss.at[s, o - 1, 0], xb_rs.at[s, o - 1], x_peer(o, 0)))
            out.append(copy(tb.at[s, x], tb.at[s, x], xb_ss.at[s, o - 1, 1], xb_rs.at[s, o - 1], x_peer(o, 1)))
        return out + [copy(xb.at[s], tb.at[s, x], xb_ss.at[s, 3, 0], xb_rs.at[s, 3], sibling(0))]

    def start(copies):
        for c in copies:
            c.start()

    def sent(copies):
        for c in copies:
            c.wait_send()

    def arrived(sems, like):
        for r in sems:
            pltpu.make_async_copy(like, like, r).wait()

    def by_core(f):
        pl.when(worker)(lambda: f(0))
        pl.when(hub)(lambda: f(1))

    both = [(i, c) for i in range(3) for c in (0, 1)] + [(3, 0)]

    loads = [
        pltpu.make_async_copy(src, dst, in_sem.at[i])
        for i, (src, dst) in enumerate((
            (rows_hbm, rows_ref), (cols_hbm, cols_ref), (cnt_hbm, cnt_ref), (mask_hbm, mask_ref),
        ))
    ] + [
        pltpu.make_async_copy(blocks_ref.at[k], blk.at[k], blk_sem.at[k])
        for k in (*range(BAND, SLOTS), *range(BAND))
    ]
    start(loads)

    barrier = pltpu.get_barrier_semaphore()

    def greet(c):
        if c == 0:
            peers = (
                [sibling(1), step_peer(7)] + [x_peer(o, 1) for o in range(1, 4)]
                + [y_peer(o, 1) for o in range(1, 4)] + [z_peer(o, 1) for o in (1, 2, 4, 6, 7)]
            )
        else:
            peers = (
                [sibling(0), step_peer(1)] + [z_peer(o, 1) for o in range(1, 8)]
                + [x_peer(o, d) for o in range(1, 4) for d in (0, 1)]
                + [y_peer(o, d) for o in range(1, 4) for d in (0, 1)]
                + [z_peer(o, 0) for o in (1, 2, 4, 6, 7)]
            )
        return peers

    def signal_peers(c):
        for dev in greet(c):
            pl.semaphore_signal(barrier, inc=1, device_id=dev, device_id_type=MESH)

    by_core(signal_peers)
    for c in loads[:4]:
        c.wait()

    live = cnt_ref[0]
    row_l = [lax.rem(rows_ref[k], RB) for k in range(SLOTS)]
    col_l = [cols_ref[k] - row * RB for k in range(BAND)]
    here = [(c >= 0) & (c < RB) for c in col_l]
    lane = lax.broadcasted_iota(jnp.int32, (8, 128), 1)
    iota8 = lax.broadcasted_iota(jnp.int32, (8, BS), 0)
    iota16 = lax.broadcasted_iota(jnp.int32, (RB, BS), 0)
    iota24 = lax.broadcasted_iota(jnp.int32, (RB + 8, BS), 0)

    idv = jnp.zeros((8, 128), jnp.int32)
    for k in range(IR_MAX):
        code = jnp.where(k < live, cols_ref[BAND + k] + 1, 0)
        idv = jnp.where(lane == yc * 8 + k, code, idv)
    ids[yc] = idv
    for q in range(4):
        keep[:, q * 128:(q + 1) * 128] = mask_ref[pl.ds(q, RB, stride=4), :].astype(F32)
    tbuf[0] = jnp.full((RB, BS), 4.0, F32)
    uloc[...] = jnp.zeros_like(uloc)

    def total_of(v):
        return jnp.sum(jnp.sum(v, axis=1, keepdims=True), axis=0, keepdims=True)

    sub = lax.broadcasted_iota(jnp.int32, (8, 128), 0)
    stat[...] = jnp.where(sub == 0, total_of(keep[...]), 0.0)

    def add_share(s, v):
        stat[...] += jnp.where(sub == s + 1, total_of(v), 0.0)

    def weights(s):
        u = jnp.where(keep[...] > 0, 4.0 / tbuf[s], 0.0)
        ubuf[s] = u
        tab[s, own] = u
        uloc[0:RB] = u
        ulast[s] = u[RB - 1:]

    def inter_columns(s):
        m = full_max(uloc[0:RB])
        inv = 1.0 / m
        acc = None
        for k in range(IR_MAX):
            vec = uloc[pl.ds(row_l[BAND + k], 1), :] * inv
            target = jnp.where(k < live, k, -1)
            lhs = split2(jnp.where(iota8 == target, vec, 0.0))
            part = jnp.dot(lhs, blk[BAND + k], preferred_element_type=F32)
            acc = part if acc is None else acc + part
        cparts[s, mine] = (acc[:8] + acc[8:]) * m

    def band_columns(s):
        m = full_max(uloc[0:RB])
        inv = 1.0 / m
        acc = None
        for k in range(BAND):
            vec = uloc[pl.ds(row_l[k], 1), :] * inv
            target = jnp.where(here[k], col_l[k], RB)
            lhs = split2(jnp.where(iota24 == target, vec, 0.0))
            part = jnp.dot(lhs, blk[k], preferred_element_type=F32)
            acc = part if acc is None else acc + part
        acc = (acc[:RB + 8] + acc[RB + 8:]) * m
        colband[...] = acc[:RB]
        pprev[s] = acc[RB:RB + 1]

    def first_columns():
        for c in loads[4:4 + IR_MAX]:
            c.wait()
        inter_columns(0)

    early = z < 4
    weights(0)

    @pl.when(early)
    def _():
        first_columns()

    def open_up(c):
        pl.semaphore_wait(barrier, len(greet(c)))
        start(tab_copies(0, c))
        up_copy(0).start()
        start(ids_copies(c))

    by_core(open_up)

    @pl.when(jnp.logical_not(early))
    def _():
        first_columns()

    by_core(lambda c: start(cp_copies(0, c)))
    for c in loads[4 + IR_MAX:]:
        c.wait()
    band_columns(0)
    pp_copy(0).start()

    def sweep(s, carry):
        last = s == SWEEPS - 1

        up_copy(s).wait_recv()
        uloc[RB:RB + 1] = uprev[s]
        m = full_max(uloc[...])
        inv = 1.0 / m
        acc = None
        for k in range(BAND):
            vec = uloc[pl.ds(jnp.where(here[k], col_l[k], RB), 1), :] * inv
            lhs = split2(jnp.where(iota16 == row_l[k], vec, 0.0))
            part = lax.dot_general(
                lhs, blk[k], (((1,), (1,)), ((), ())), preferred_element_type=F32
            )
            acc = part if acc is None else acc + part
        rowband[...] = (acc[:RB] + acc[RB:]) * m

        @pl.when(worker)
        def _():
            add_share(s, uloc[0:RB] * rowband[...])

            @pl.when(last)
            def _():
                copy(stat, wstat, ws_ss, ws_rs, sibling(1)).start()

        @pl.when(hub)
        def _():
            @pl.when(s == 0)
            def _():
                arrived([ids_rs.at[i, c] for i, c in both], ids.at[0])
                code = ids[0]
                for p in range(1, 8):
                    code = code + ids[p]
                code = code[0:1]
                cc = jnp.maximum(code - 1, 0)
                want = jnp.where(
                    (code > 0) & (((cc // 32) % 4) == y), (cc // 128) * 32 + cc % 32, -1
                )
                full = jnp.where(
                    lax.broadcasted_iota(jnp.int32, (128, 128), 0) == want, 1.0, 0.0
                )
                pick[...] = full[:, :SEL].astype(BF16)
                pickt[...] = full.T[:SEL].astype(BF16)

            arrived([tab_rs.at[s, i, c] for i, c in both], tab.at[s, own])
            selm[s] = exact_pick(pickt[...], tab[s])
            start(sel_copies(s))
            rsel[s, y] = selm[s, mine]

            arrived([cp_rs.at[s, i, c] for i, c in both], cparts.at[s, mine])
            dense[s] = exact_pick(pick[...], cparts[s])
            start(dz_copies(s))
            rz[s, 3] = dense[s, own]

            @pl.when(last)
            def _():
                arrived([ws_rs], wstat)
                add_share(s, dense[s] * tab[s])
                add_share(s, uloc[0:RB] * rowband[...])
                stz[z] = stat[...] + wstat[...]
                for o in range(1, 8):
                    copy(stz.at[z], stz.at[z], sz_ss.at[o - 1], sz_rs.at[o - 1], z_peer(o, 1)).start()

        arrived([sel_rs.at[s, i] for i in range(3)], rsel.at[s, 0])
        pl.when(worker)(lambda: arrived([sel_rs.at[s, 3]], rsel.at[s, 0]))
        ucol = (rsel[s, 0] + rsel[s, 1]) + (rsel[s, 2] + rsel[s, 3])
        m2 = full_max(ucol)
        ucol = ucol * (1.0 / m2)
        acc = None
        for k in range(IR_MAX):
            target = jnp.where(k < live, row_l[BAND + k], -1)
            lhs = split2(jnp.where(iota16 == target, ucol[k:k + 1], 0.0))
            part = lax.dot_general(
                lhs, blk[BAND + k], (((1,), (1,)), ((), ())), preferred_element_type=F32
            )
            acc = part if acc is None else acc + part
        total = (acc[:RB] + acc[RB:]) * m2 + rowband[...] + colband[...]

        pp_copy(s).wait_recv()
        total = total + jnp.where(iota16 == RB - 1, prevp[s], 0.0)
        arrived([dz_rs.at[s, i] for i in range(3)], rz.at[s, 0])
        pl.when(worker)(lambda: arrived([dz_rs.at[s, 3]], rz.at[s, 0]))
        total = total + ((rz[s, 0] + rz[s, 1]) + (rz[s, 2] + rz[s, 3]))

        zb[s, core, 0] = total[:, half:]
        by_core(lambda c: start(zb_copies(s, c)))
        xa[s, core, x] = total[:, :half]
        by_core(lambda c: start(xa_copies(s, c)))

        @pl.when(worker)
        def _():
            sent([*tab_copies(s, 0), up_copy(s), *cp_copies(s, 0), pp_copy(s)])

        @pl.when(hub)
        def _():
            @pl.when(jnp.logical_not(last))
            def _():
                add_share(s, dense[s] * tab[s])
                add_share(s, uloc[0:RB] * rowband[...])

            @pl.when(last)
            def _():
                for o in range(1, 8):
                    copy(stz.at[z], stz.at[z], sz_ss.at[o - 1], sz_rs.at[o - 1], z_peer(o, 1)).wait()
                v = stz[0]
                for p in range(1, 8):
                    v = v + stz[p]
                sty[y] = v
                for o in RING:
                    copy(sty.at[y], sty.at[y], sy_ss.at[o - 1], sy_rs.at[o - 1], y_peer(o, 1)).start()

            sent([*tab_copies(s, 1), up_copy(s), *cp_copies(s, 1), pp_copy(s), *sel_copies(s), *dz_copies(s)])

            arrived([xa_rs.at[s, i, c] for i, c in both], xa.at[s, 0, 0])
            za[s] = (xa[s, 0, 0] + xa[s, 0, 1]) + (xa[s, 0, 2] + xa[s, 0, 3])
            ta[s, 0] = (xa[s, 1, 0] + xa[s, 1, 1]) + (xa[s, 1, 2] + xa[s, 1, 3])
            start(za_copies(s))
            arrived([zb_rs.at[s, 0, 0], zb_rs.at[s, 0, 1], zb_rs.at[s, 1, 0]], zb.at[s, 0, 0])
            xb[s] = zb[s, 0, 0] + zb[s, 0, 1]
            tb[s, x] = zb[s, 1, 0] + zb[s, 1, 1]
            start(xb_copies(s))

            @pl.when(last)
            def _():
                for o in RING:
                    copy(sty.at[y], sty.at[y], sy_ss.at[o - 1], sy_rs.at[o - 1], y_peer(o, 1)).wait()
                stx[x] = (sty[0] + sty[1]) + (sty[2] + sty[3])
                for o in RING:
                    copy(stx.at[x], stx.at[x], sx_ss.at[o - 1], sx_rs.at[o - 1], x_peer(o, 1)).start()

            sent([*za_copies(s), *xb_copies(s)])

        by_core(lambda c: sent([*xa_copies(s, c), *zb_copies(s, c)]))
        arrived([xb_rs.at[s, i] for i in range(3)], tb.at[s, 0])
        pl.when(worker)(lambda: arrived([xb_rs.at[s, 3], za_rs.at[s, 0]], tb.at[s, 0]))
        arrived([za_rs.at[s, 1]], tb.at[s, 0])
        tbuf[s + 1, :, :half] = ta[s, 0] + ta[s, 1]
        tbuf[s + 1, :, half:] = (tb[s, 0] + tb[s, 1]) + (tb[s, 2] + tb[s, 3])

        @pl.when(s < SWEEPS - 1)
        def _():
            n = s + 1
            weights(n)
            by_core(lambda c: start(tab_copies(n, c)))
            up_copy(n).start()
            inter_columns(n)
            by_core(lambda c: start(cp_copies(n, c)))
            band_columns(n)
            pp_copy(n).start()

        return carry

    lax.fori_loop(0, SWEEPS, sweep, 0)

    @pl.when(hub)
    def _():
        for o in RING:
            copy(stx.at[x], stx.at[x], sx_ss.at[o - 1], sx_rs.at[o - 1], x_peer(o, 1)).wait()
        fin[...] = (stx[0] + stx[1]) + (stx[2] + stx[3])
        c = copy(fin, fin, fin_ss, fin_rs, sibling(0))
        c.start()
        c.wait_send()
        sent(ids_copies(1))

    @pl.when(worker)
    def _():
        sent([copy(stat, wstat, ws_ss, ws_rs, sibling(1)), *ids_copies(0)])
        arrived([fin_rs], fin)

    v = fin[...]
    count = v[0:1, 0:1] * 0.125
    mean1 = v[1:2, 0:1] * 2.0 / count
    mean2 = v[2:3, 0:1] * 2.0 / count
    mean3 = v[3:4, 0:1] * 2.0 / count
    scale = mean1 * mean2 * 0.0625 * mean3
    b3 = tbuf[SWEEPS]
    bias = jnp.where(keep[...] > 0, b3 / scale, 1.0)
    balance = b3 * ubuf[SWEEPS - 1] / mean3
    for q in range(4):
        bias_ref[pl.ds(q, RB, stride=4), :] = bias[:, q * 128:(q + 1) * 128]
        bal_ref[pl.ds(q, RB, stride=4), :] = balance[:, q * 128:(q + 1) * 128]


def body(blocks, block_rows, block_cols, inter_counts, keep_mask):
    seg = keep_mask.shape[0]
    vm = pl.BlockSpec(memory_space=pltpu.VMEM)
    hbm = pl.BlockSpec(memory_space=pl.ANY)
    S = SWEEPS
    H = BS // 2
    dma = pltpu.SemaphoreType.DMA
    i32 = jnp.int32
    out = jax.ShapeDtypeStruct((seg // 128, 128), F32)

    def vf(*shape):
        return pltpu.VMEM(shape, F32)

    bias, balance = pl.pallas_call(
        kernel,
        out_shape=(out, out),
        in_specs=[hbm] * 5,
        out_specs=(vm, vm),
        scratch_shapes=[
            pltpu.SMEM((SLOTS,), i32),
            pltpu.SMEM((SLOTS,), i32),
            pltpu.SMEM((1,), i32),
            pltpu.VMEM((seg // 128, 128), i32),
            pltpu.VMEM((SLOTS, BS, BS), BF16),
            vf(RB, BS),
            vf(S + 1, RB, BS),
            vf(S, RB, BS),
            vf(RB + 8, BS),
            pltpu.VMEM((8, 8, 128), i32),
            pltpu.VMEM((128, SEL), BF16),
            pltpu.VMEM((SEL, 128), BF16),
            vf(8, 128),
            vf(RB, BS),
            vf(RB, BS),
            vf(S, 128, BS),
            vf(S, SEL, BS),
            vf(S, 4, 8, BS),
            vf(S, 1, BS),
            vf(S, 1, BS),
            vf(S, SEL, BS),
            vf(S, 1, BS),
            vf(S, 1, BS),
            vf(S, 128, BS),
            vf(S, 4, RB, BS),
            vf(S, 2, 4, RB, H),
            vf(S, RB, H),
            vf(S, 2, RB, H),
            vf(S, 2, 2, RB, H),
            vf(S, RB, H),
            vf(S, 4, RB, H),
            vf(8, 128),
            vf(8, 8, 128),
            vf(4, 8, 128),
            vf(4, 8, 128),
            vf(8, 128),
            dma((4,)),
            dma((SLOTS,)),
            dma((4,)), dma((4, 2)),
            dma((S, 4)), dma((S, 4, 2)),
            dma((S, 4, 2)), dma((S, 4)),
            dma((S,)), dma((S,)),
            dma((S, 4)), dma((S, 4, 2)),
            dma((S,)), dma((S,)),
            dma((S, 4, 2)), dma((S, 4)),
            dma((S, 4)), dma((S, 4, 2)),
            dma((S, 3)), dma((S, 2)),
            dma((S, 2)), dma((S, 2, 2)),
            dma((S, 4, 2)), dma((S, 4)),
            dma, dma,
            dma((7,)), dma((7,)),
            dma((3,)), dma((3,)),
            dma((3,)), dma((3,)),
            dma, dma,
        ],
        compiler_params=pltpu.CompilerParams(
            collective_id=0, has_side_effects=True, vmem_limit_bytes=VMEM_LIMIT
        ),
        name="balance",
    )(block_rows, block_cols, inter_counts, keep_mask.reshape(seg // 128, 128), blocks)
    return bias.reshape(seg), balance.reshape(seg)


def solution(mesh):
    return jax.shard_map(
        body,
        mesh=mesh,
        in_specs=(
            P(("row", "col"), None, None),
            P(("row", "col")),
            P(("row", "col")),
            P(("row", "col")),
            P("row"),
        ),
        out_specs=(P("row"), P("row")),
        check_vma=False,
    )
```

time: 74.3 us -> 67.5 us (0.908)
  Pallas kernels: 69.3 us -> 63.2 us
    pallas_call x1, Pallas kernels: 69.3 us -> 63.2 us  [body(): pl.pallas_call(kernel, out_shape=(out, out), in_specs=[hbm] * 5, out_spec...]
    unnamed x8 -> x2, local copies, waits for them, and re-layouts: 3.3 us -> 2.75 us
where the time goes in v4:
time: 67.5 us; the launch traced here: 67.2 us
  Pallas kernels  63.2 us (94%)
  local copies, waits for them, and re-layouts  2.75 us (4%)
  between operations  1.29 us (2%)
    pallas_call x1, Pallas kernels, body(): pl.pallas_call(kernel, out_shape=(out, out), in_specs=[hbm] * 5, out_spec...  63.2 us
    unnamed x2, local copies, waits for them, and re-layouts  2.75 us

profile of v4, /device:TPU:1, one launch (start us, length us, event | category | flops | bytes accessed | tf_op | source)
XLA Modules:
  0.0 67.2 jit_solution(3346879011865619855)
XLA Ops:
  1.3 63.2 %balance.1 = (f32[64,128]{1,0:T(8,128)}, f32[64,128]{1,0:T(8,128)}) custom-call(s32[12]{0:T(128)} %rows_hbm.1, s32[12]{0:T(128)} %cols_hbm.1, s32[1]{0:T(128)S(6)} %copy.9.cnt_hbm, s32[64,128]{1,0:T(8,128)} %bitcast.3, bf16[12,512,512]{2,1,0:T(8,128)(2,1)} %blocks_ref.1), custom_call_target="tpu_custom_call" | custom-call | tf_op jit(solution)/shard_map/balance/pallas_call | solution.py:522
  64.5 1.4 %copy.10 = f32[8192]{0:T(1024)} copy(f32[8192]{0:T(1024)} %bitcast.5) | data formatting | bytes 65536
  65.9 1.4 %copy.11 = f32[8192]{0:T(1024)} copy(f32[8192]{0:T(1024)} %bitcast.4) | data formatting | bytes 65536

commit v5 on v4

--- a/solution.py
+++ b/solution.py
@@ -26,14 +26,10 @@
     return jnp.concatenate([hi, lo], axis=0)
 
 
-def exact_pick(pick, v):
-    out = None
-    for _ in range(3):
-        term = v.astype(BF16)
-        v = v - term.astype(F32)
-        part = jnp.dot(pick, term, preferred_element_type=F32)
-        out = part if out is None else out + part
-    return out
+def two_term_pick(pick, v):
+    hi = v.astype(BF16)
+    lo = (v - hi.astype(F32)).astype(BF16)
+    return jnp.dot(pick, hi, preferred_element_type=F32) + jnp.dot(pick, lo, preferred_element_type=F32)
 
 
 def full_max(v):
@@ -43,15 +39,15 @@
 
 def kernel(
     rows_hbm, cols_hbm, cnt_hbm, mask_hbm, blocks_ref,
-    bias_ref, bal_ref,
+    out_ref,
     rows_ref, cols_ref, cnt_ref, mask_ref,
-    blk, keep, tbuf, ubuf, uloc, ids, pick, pickt, stat, rowband, colband,
+    blk, blkt, keep, tbuf, ubuf, uloc, ids, pick, pickt, stat, rowband, colband,
     tab, selm, rsel, ulast, uprev, cparts, pprev, prevp, dense, rz,
-    xa, za, ta, zb, xb, tb, wstat, stz, sty, stx, fin,
+    xa, za, ta, zb, xb, tb, wstat, stz, sty, stx,
     in_sem, blk_sem, ids_ss, ids_rs, tab_ss, tab_rs, sel_ss, sel_rs, up_ss, up_rs,
     cp_ss, cp_rs, pp_ss, pp_rs, dz_ss, dz_rs, xa_ss, xa_rs, za_ss, za_rs,
     zb_ss, zb_rs, xb_ss, xb_rs, ws_ss, ws_rs,
-    sz_ss, sz_rs, sy_ss, sy_rs, sx_ss, sx_rs, fin_ss, fin_rs,
+    sz_ss, sz_rs, sy_ss, sy_rs, sx_ss, sx_rs,
 ):
     row = lax.axis_index("row")
     col = lax.axis_index("col")
@@ -178,6 +174,13 @@
             out.append(copy(tb.at[s, x], tb.at[s, x], xb_ss.at[s, o - 1, 1], xb_rs.at[s, o - 1], x_peer(o, 1)))
         return out + [copy(xb.at[s], tb.at[s, x], xb_ss.at[s, 3, 0], xb_rs.at[s, 3], sibling(0))]
 
+    def sx_copies():
+        out = [
+            copy(stx.at[x], stx.at[x], sx_ss.at[o - 1, c], sx_rs.at[o - 1], x_peer(o, c))
+            for o in RING for c in (0, 1)
+        ]
+        return out + [copy(stx.at[x], stx.at[x], sx_ss.at[3, 0], sx_rs.at[3], sibling(0))]
+
     def start(copies):
         for c in copies:
             c.start()
@@ -298,12 +301,20 @@
             c.wait()
         inter_columns(0)
 
+    def transpose_inter():
+        def one(k, carry):
+            blkt[k] = blk[BAND + k].T
+            return carry
+
+        lax.fori_loop(0, IR_MAX, one, 0)
+
     early = z < 4
     weights(0)
 
     @pl.when(early)
     def _():
         first_columns()
+        transpose_inter()
 
     def open_up(c):
         pl.semaphore_wait(barrier, len(greet(c)))
@@ -322,6 +333,10 @@
         c.wait()
     band_columns(0)
     pp_copy(0).start()
+
+    @pl.when(jnp.logical_not(early))
+    def _():
+        transpose_inter()
 
     def sweep(s, carry):
         last = s == SWEEPS - 1
@@ -368,12 +383,12 @@
                 pickt[...] = full.T[:SEL].astype(BF16)
 
             arrived([tab_rs.at[s, i, c] for i, c in both], tab.at[s, own])
-            selm[s] = exact_pick(pickt[...], tab[s])
+            selm[s] = two_term_pick(pickt[...], tab[s])
             start(sel_copies(s))
             rsel[s, y] = selm[s, mine]
 
             arrived([cp_rs.at[s, i, c] for i, c in both], cparts.at[s, mine])
-            dense[s] = exact_pick(pick[...], cparts[s])
+            dense[s] = two_term_pick(pick[...], cparts[s])
             start(dz_copies(s))
             rz[s, 3] = dense[s, own]
 
@@ -395,9 +410,7 @@
         for k in range(IR_MAX):
             target = jnp.where(k < live, row_l[BAND + k], -1)
             lhs = split2(jnp.where(iota16 == target, ucol[k:k + 1], 0.0))
-            part = lax.dot_general(
-                lhs, blk[BAND + k], (((1,), (1,)), ((), ())), preferred_element_type=F32
-            )
+            part = jnp.dot(lhs, blkt[k], preferred_element_type=F32)
             acc = part if acc is None else acc + part
         total = (acc[:RB] + acc[RB:]) * m2 + rowband[...] + colband[...]
 
@@ -450,8 +463,7 @@
                 for o in RING:
                     copy(sty.at[y], sty.at[y], sy_ss.at[o - 1], sy_rs.at[o - 1], y_peer(o, 1)).wait()
                 stx[x] = (sty[0] + sty[1]) + (sty[2] + sty[3])
-                for o in RING:
-                    copy(stx.at[x], stx.at[x], sx_ss.at[o - 1], sx_rs.at[o - 1], x_peer(o, 1)).start()
+                start(sx_copies())
 
             sent([*za_copies(s), *xb_copies(s)])
 
@@ -477,22 +489,18 @@
 
     lax.fori_loop(0, SWEEPS, sweep, 0)
 
+    arrived([sx_rs.at[i] for i in range(3)], stx.at[0])
+
     @pl.when(hub)
     def _():
-        for o in RING:
-            copy(stx.at[x], stx.at[x], sx_ss.at[o - 1], sx_rs.at[o - 1], x_peer(o, 1)).wait()
-        fin[...] = (stx[0] + stx[1]) + (stx[2] + stx[3])
-        c = copy(fin, fin, fin_ss, fin_rs, sibling(0))
-        c.start()
-        c.wait_send()
-        sent(ids_copies(1))
+        sent([*ids_copies(1), *sx_copies()])
 
     @pl.when(worker)
     def _():
         sent([copy(stat, wstat, ws_ss, ws_rs, sibling(1)), *ids_copies(0)])
-        arrived([fin_rs], fin)
-
-    v = fin[...]
+        arrived([sx_rs.at[3]], stx.at[0])
+
+    v = (stx[0] + stx[1]) + (stx[2] + stx[3])
     count = v[0:1, 0:1] * 0.125
     mean1 = v[1:2, 0:1] * 2.0 / count
     mean2 = v[2:3, 0:1] * 2.0 / count
@@ -502,8 +510,8 @@
     bias = jnp.where(keep[...] > 0, b3 / scale, 1.0)
     balance = b3 * ubuf[SWEEPS - 1] / mean3
     for q in range(4):
-        bias_ref[pl.ds(q, RB, stride=4), :] = bias[:, q * 128:(q + 1) * 128]
-        bal_ref[pl.ds(q, RB, stride=4), :] = balance[:, q * 128:(q + 1) * 128]
+        out_ref[pl.ds(q, RB, stride=4), :] = bias[:, q * 128:(q + 1) * 128]
+        out_ref[pl.ds(4 * RB + q, RB, stride=4), :] = balance[:, q * 128:(q + 1) * 128]
 
 
 def body(blocks, block_rows, block_cols, inter_counts, keep_mask):
@@ -514,22 +522,23 @@
     H = BS // 2
     dma = pltpu.SemaphoreType.DMA
     i32 = jnp.int32
-    out = jax.ShapeDtypeStruct((seg // 128, 128), F32)
+    out = jax.ShapeDtypeStruct((seg // 64, 128), F32)
 
     def vf(*shape):
         return pltpu.VMEM(shape, F32)
 
-    bias, balance = pl.pallas_call(
+    both = pl.pallas_call(
         kernel,
-        out_shape=(out, out),
+        out_shape=out,
         in_specs=[hbm] * 5,
-        out_specs=(vm, vm),
+        out_specs=vm,
         scratch_shapes=[
             pltpu.SMEM((SLOTS,), i32),
             pltpu.SMEM((SLOTS,), i32),
             pltpu.SMEM((1,), i32),
             pltpu.VMEM((seg // 128, 128), i32),
             pltpu.VMEM((SLOTS, BS, BS), BF16),
+            pltpu.VMEM((IR_MAX, BS, BS), BF16),
             vf(RB, BS),
             vf(S + 1, RB, BS),
             vf(S, RB, BS),
@@ -560,7 +569,6 @@
             vf(8, 8, 128),
             vf(4, 8, 128),
             vf(4, 8, 128),
-            vf(8, 128),
             dma((4,)),
             dma((SLOTS,)),
             dma((4,)), dma((4, 2)),
@@ -577,14 +585,14 @@
             dma, dma,
             dma((7,)), dma((7,)),
             dma((3,)), dma((3,)),
-            dma((3,)), dma((3,)),
-            dma, dma,
+            dma((4, 2)), dma((4,)),
         ],
         compiler_params=pltpu.CompilerParams(
             collective_id=0, has_side_effects=True, vmem_limit_bytes=VMEM_LIMIT
         ),
         name="balance",
     )(block_rows, block_cols, inter_counts, keep_mask.reshape(seg // 128, 128), blocks)
+    bias, balance = both[:seg // 128], both[seg // 128:]
     return bias.reshape(seg), balance.reshape(seg)
 
 

time: 67.5 us -> 63.8 us (0.945)
  Pallas kernels: 63.2 us -> 60.9 us
  local copies, waits for them, and re-layouts: 2.75 us -> 1.4 us
    unnamed x2 -> x0, local copies, waits for them, and re-layouts: 2.75 us -> none
    pallas_call x1, Pallas kernels: 63.2 us -> 60.9 us  [body(): pl.pallas_call(kernel, out_shape=out, in_specs=[hbm] * 5, out_specs=vm, s...]
    reshape x0 -> x1, local copies, waits for them, and re-layouts: none -> 1.4 us  [body(): return (bias.reshape(seg), balance.reshape(seg))]
where the time goes in v5:
time: 63.8 us; the launch traced here: 63.6 us
  Pallas kernels  60.9 us (95%)
  local copies, waits for them, and re-layouts  1.4 us (2%)
  between operations  1.28 us (2%)
    pallas_call x1, Pallas kernels, body(): pl.pallas_call(kernel, out_shape=out, in_specs=[hbm] * 5, out_specs=vm, s...  60.9 us
    reshape x1, local copies, waits for them, and re-layouts, body(): return (bias.reshape(seg), balance.reshape(seg))  1.4 us

profile of v5, /device:TPU:1, one launch (start us, length us, event | category | flops | bytes accessed | tf_op | source)
XLA Modules:
  0.0 63.6 jit_solution(13331284588666726021)
XLA Ops:
  1.3 60.9 %balance.1 = f32[128,128]{1,0:T(8,128)} custom-call(s32[12]{0:T(128)} %rows_hbm.1, s32[12]{0:T(128)} %cols_hbm.1, s32[1]{0:T(128)S(6)} %copy.7.cnt_hbm, s32[64,128]{1,0:T(8,128)} %bitcast.5, bf16[12,512,512]{2,1,0:T(8,128)(2,1)} %blocks_ref.1), custom_call_target="tpu_custom_call" | custom-call | tf_op jit(solution)/shard_map/balance/pallas_call | solution.py:530
  62.2 1.4 %slice_bitcast_fusion = (f32[8192]{0:T(1024)}, f32[8192]{0:T(1024)}) fusion(f32[128,128]{1,0:T(8,128)} %balance.1), kind=kLoop, calls=%fused_computation | loop fusion | bytes 131072 | tf_op jit(solution)/shard_map/reshape | solution.py:596

commit v6 on v5

--- a/solution.py
+++ b/solution.py
@@ -208,22 +208,22 @@
         pltpu.make_async_copy(blocks_ref.at[k], blk.at[k], blk_sem.at[k])
         for k in (*range(BAND, SLOTS), *range(BAND))
     ]
-    start(loads)
+    loads[3].start()
 
     barrier = pltpu.get_barrier_semaphore()
 
     def greet(c):
         if c == 0:
             peers = (
-                [sibling(1), step_peer(7)] + [x_peer(o, 1) for o in range(1, 4)]
-                + [y_peer(o, 1) for o in range(1, 4)] + [z_peer(o, 1) for o in (1, 2, 4, 6, 7)]
+                [z_peer(o, 1) for o in (2, 6, 1, 7)] + [y_peer(o, 1) for o in RING]
+                + [x_peer(o, 1) for o in RING] + [sibling(1), step_peer(7)]
             )
         else:
             peers = (
-                [sibling(0), step_peer(1)] + [z_peer(o, 1) for o in range(1, 8)]
-                + [x_peer(o, d) for o in range(1, 4) for d in (0, 1)]
-                + [y_peer(o, d) for o in range(1, 4) for d in (0, 1)]
-                + [z_peer(o, 0) for o in (1, 2, 4, 6, 7)]
+                [z_peer(o, d) for o in (2, 6, 1, 7) for d in (0, 1)]
+                + [y_peer(o, d) for o in RING for d in (0, 1)]
+                + [x_peer(o, d) for o in RING for d in (0, 1)]
+                + [sibling(0), step_peer(1)]
             )
         return peers
 
@@ -232,6 +232,7 @@
             pl.semaphore_signal(barrier, inc=1, device_id=dev, device_id_type=MESH)
 
     by_core(signal_peers)
+    start([*loads[:3], *loads[4:]])
     for c in loads[:4]:
         c.wait()
 
@@ -296,11 +297,6 @@
         colband[...] = acc[:RB]
         pprev[s] = acc[RB:RB + 1]
 
-    def first_columns():
-        for c in loads[4:4 + IR_MAX]:
-            c.wait()
-        inter_columns(0)
-
     def transpose_inter():
         def one(k, carry):
             blkt[k] = blk[BAND + k].T
@@ -308,38 +304,36 @@
 
         lax.fori_loop(0, IR_MAX, one, 0)
 
-    early = z < 4
-    weights(0)
-
-    @pl.when(early)
-    def _():
-        first_columns()
-        transpose_inter()
-
     def open_up(c):
         pl.semaphore_wait(barrier, len(greet(c)))
-        start(tab_copies(0, c))
-        up_copy(0).start()
         start(ids_copies(c))
 
     by_core(open_up)
 
-    @pl.when(jnp.logical_not(early))
-    def _():
-        first_columns()
-
-    by_core(lambda c: start(cp_copies(0, c)))
-    for c in loads[4 + IR_MAX:]:
-        c.wait()
-    band_columns(0)
-    pp_copy(0).start()
-
-    @pl.when(jnp.logical_not(early))
-    def _():
-        transpose_inter()
-
     def sweep(s, carry):
+        first = s == 0
         last = s == SWEEPS - 1
+
+        weights(s)
+        by_core(lambda c: start(tab_copies(s, c)))
+        up_copy(s).start()
+
+        @pl.when(first)
+        def _():
+            for c in loads[4:4 + IR_MAX]:
+                c.wait()
+
+        inter_columns(s)
+        by_core(lambda c: start(cp_copies(s, c)))
+
+        @pl.when(first)
+        def _():
+            for c in loads[4 + IR_MAX:]:
+                c.wait()
+
+        band_columns(s)
+        pp_copy(s).start()
+        pl.when(first)(transpose_inter)
 
         up_copy(s).wait_recv()
         uloc[RB:RB + 1] = uprev[s]
@@ -365,7 +359,7 @@
 
         @pl.when(hub)
         def _():
-            @pl.when(s == 0)
+            @pl.when(first)
             def _():
                 arrived([ids_rs.at[i, c] for i, c in both], ids.at[0])
                 code = ids[0]
@@ -453,10 +447,6 @@
             za[s] = (xa[s, 0, 0] + xa[s, 0, 1]) + (xa[s, 0, 2] + xa[s, 0, 3])
             ta[s, 0] = (xa[s, 1, 0] + xa[s, 1, 1]) + (xa[s, 1, 2] + xa[s, 1, 3])
             start(za_copies(s))
-            arrived([zb_rs.at[s, 0, 0], zb_rs.at[s, 0, 1], zb_rs.at[s, 1, 0]], zb.at[s, 0, 0])
-            xb[s] = zb[s, 0, 0] + zb[s, 0, 1]
-            tb[s, x] = zb[s, 1, 0] + zb[s, 1, 1]
-            start(xb_copies(s))
 
             @pl.when(last)
             def _():
@@ -465,6 +455,11 @@
                 stx[x] = (sty[0] + sty[1]) + (sty[2] + sty[3])
                 start(sx_copies())
 
+            arrived([zb_rs.at[s, 0, 0], zb_rs.at[s, 0, 1], zb_rs.at[s, 1, 0]], zb.at[s, 0, 0])
+            xb[s] = zb[s, 0, 0] + zb[s, 0, 1]
+            tb[s, x] = zb[s, 1, 0] + zb[s, 1, 1]
+            start(xb_copies(s))
+
             sent([*za_copies(s), *xb_copies(s)])
 
         by_core(lambda c: sent([*xa_copies(s, c), *zb_copies(s, c)]))
@@ -473,17 +468,6 @@
         arrived([za_rs.at[s, 1]], tb.at[s, 0])
         tbuf[s + 1, :, :half] = ta[s, 0] + ta[s, 1]
         tbuf[s + 1, :, half:] = (tb[s, 0] + tb[s, 1]) + (tb[s, 2] + tb[s, 3])
-
-        @pl.when(s < SWEEPS - 1)
-        def _():
-            n = s + 1
-            weights(n)
-            by_core(lambda c: start(tab_copies(n, c)))
-            up_copy(n).start()
-            inter_columns(n)
-            by_core(lambda c: start(cp_copies(n, c)))
-            band_columns(n)
-            pp_copy(n).start()
 
         return carry
 

time: 63.8 us -> 62.7 us (0.983)
  Pallas kernels: 60.9 us -> 59.9 us
    pallas_call x1, Pallas kernels: 60.9 us -> 59.9 us  [body(): pl.pallas_call(kernel, out_shape=out, in_specs=[hbm] * 5, out_specs=vm, s...]
where the time goes in v6:
time: 62.7 us; the launch traced here: 62.5 us
  Pallas kernels  59.9 us (96%)
  local copies, waits for them, and re-layouts  1.4 us (2%)
  between operations  1.28 us (2%)
    pallas_call x1, Pallas kernels, body(): pl.pallas_call(kernel, out_shape=out, in_specs=[hbm] * 5, out_specs=vm, s...  59.9 us
    reshape x1, local copies, waits for them, and re-layouts, body(): return (bias.reshape(seg), balance.reshape(seg))  1.4 us

profile of v6, /device:TPU:1, one launch (start us, length us, event | category | flops | bytes accessed | tf_op | source)
XLA Modules:
  0.0 62.5 jit_solution(3140490352039314193)
XLA Ops:
  1.3 59.9 %balance.1 = f32[128,128]{1,0:T(8,128)} custom-call(s32[12]{0:T(128)} %rows_hbm.1, s32[12]{0:T(128)} %cols_hbm.1, s32[1]{0:T(128)S(6)} %copy.7.cnt_hbm, s32[64,128]{1,0:T(8,128)} %bitcast.5, bf16[12,512,512]{2,1,0:T(8,128)(2,1)} %blocks_ref.1), custom_call_target="tpu_custom_call" | custom-call | tf_op jit(solution)/shard_map/balance/pallas_call | solution.py:514
  61.1 1.4 %slice_bitcast_fusion = (f32[8192]{0:T(1024)}, f32[8192]{0:T(1024)}) fusion(f32[128,128]{1,0:T(8,128)} %balance.1), kind=kLoop, calls=%fused_computation | loop fusion | bytes 131072 | tf_op jit(solution)/shard_map/reshape | solution.py:580

commit v7 on v6

--- a/solution.py
+++ b/solution.py
@@ -101,26 +101,26 @@
 
     def tab_copies(s, c):
         out = [
-            copy(tab.at[s, own], tab.at[s, own], tab_ss.at[s, i], tab_rs.at[s, i, c], z_peer(o, 1))
+            copy(tab.at[s, own], tab.at[s, own], tab_ss.at[s], tab_rs.at[s], z_peer(o, 1))
             for i, o in enumerate((two[c], 1, 7))
         ]
         if c == 0:
-            out.append(copy(tab.at[s, own], tab.at[s, own], tab_ss.at[s, 3], tab_rs.at[s, 3, 0], sibling(1)))
+            out.append(copy(tab.at[s, own], tab.at[s, own], tab_ss.at[s], tab_rs.at[s], sibling(1)))
         return out
 
     def ids_copies(c):
-        out = [copy(ids.at[yc], ids.at[yc], ids_ss.at[o - 1], ids_rs.at[o - 1, c], y_peer(o, 1)) for o in RING]
-        if c == 0:
-            out.append(copy(ids.at[yc], ids.at[yc], ids_ss.at[3], ids_rs.at[3, 0], sibling(1)))
+        out = [copy(ids.at[yc], ids.at[yc], ids_ss, ids_rs, y_peer(o, 1)) for o in RING]
+        if c == 0:
+            out.append(copy(ids.at[yc], ids.at[yc], ids_ss, ids_rs, sibling(1)))
         return out
 
     def cp_copies(s, c):
         out = [
-            copy(cparts.at[s, mine], cparts.at[s, mine], cp_ss.at[s, o - 1], cp_rs.at[s, o - 1, c], y_peer(o, 1))
+            copy(cparts.at[s, mine], cparts.at[s, mine], cp_ss.at[s], cp_rs.at[s], y_peer(o, 1))
             for o in RING
         ]
         if c == 0:
-            out.append(copy(cparts.at[s, mine], cparts.at[s, mine], cp_ss.at[s, 3], cp_rs.at[s, 3, 0], sibling(1)))
+            out.append(copy(cparts.at[s, mine], cparts.at[s, mine], cp_ss.at[s], cp_rs.at[s], sibling(1)))
         return out
 
     def up_copy(s):
@@ -132,72 +132,65 @@
     def sel_copies(s):
         out = [
             copy(selm.at[s, eight(lax.rem(y + o, 4) * 2 + c)], rsel.at[s, y],
-                 sel_ss.at[s, o - 1, c], sel_rs.at[s, o - 1], y_peer(o, c))
+                 sel_ss.at[s], sel_rs.at[s], y_peer(o, c))
             for o in RING for c in (0, 1)
         ]
-        return out + [copy(selm.at[s, eight(y * 2)], rsel.at[s, y], sel_ss.at[s, 3, 0], sel_rs.at[s, 3], sibling(0))]
+        return out + [copy(selm.at[s, eight(y * 2)], rsel.at[s, y], sel_ss.at[s], sel_rs.at[s], sibling(0))]
 
     def dz_copies(s):
         out = [
             copy(dense.at[s, seg(lax.rem(zl + o, 4), c)], rz.at[s, i],
-                 dz_ss.at[s, i, c], dz_rs.at[s, i], z_peer(o, c))
+                 dz_ss.at[s], dz_rs.at[s], z_peer(o, c))
             for c in (0, 1) for i, o in enumerate((two[c], 1, 7))
         ]
-        return out + [copy(dense.at[s, seg(zl, 0)], rz.at[s, 3], dz_ss.at[s, 3, 0], dz_rs.at[s, 3], sibling(0))]
+        return out + [copy(dense.at[s, seg(zl, 0)], rz.at[s, 3], dz_ss.at[s], dz_rs.at[s], sibling(0))]
 
     def xa_copies(s, c):
         out = [
-            copy(xa.at[s, c, x], xa.at[s, c, x], xa_ss.at[s, o - 1], xa_rs.at[s, o - 1, c], x_peer(o, 1))
+            copy(xa.at[s, c, x], xa.at[s, c, x], xa_ss.at[s], xa_rs.at[s, c], x_peer(o, 1))
             for o in RING
         ]
         if c == 0:
-            out.append(copy(xa.at[s, 0, x], xa.at[s, 0, x], xa_ss.at[s, 3], xa_rs.at[s, 3, 0], sibling(1)))
+            out.append(copy(xa.at[s, 0, x], xa.at[s, 0, x], xa_ss.at[s], xa_rs.at[s, c], sibling(1)))
         return out
 
     def za_copies(s):
         return [
-            copy(za.at[s], ta.at[s, 1], za_ss.at[s, 0], za_rs.at[s, 1], z_peer(4, 0)),
-            copy(ta.at[s, 0], ta.at[s, 1], za_ss.at[s, 1], za_rs.at[s, 1], z_peer(4, 1)),
-            copy(za.at[s], ta.at[s, 0], za_ss.at[s, 2], za_rs.at[s, 0], sibling(0)),
+            copy(za.at[s], ta.at[s, 1], za_ss.at[s], za_rs.at[s], z_peer(4, 0)),
+            copy(ta.at[s, 0], ta.at[s, 1], za_ss.at[s], za_rs.at[s], z_peer(4, 1)),
+            copy(za.at[s], ta.at[s, 0], za_ss.at[s], za_rs.at[s], sibling(0)),
         ]
 
     def zb_copies(s, c):
-        out = [copy(zb.at[s, c, 0], zb.at[s, c, 1], zb_ss.at[s, 0], zb_rs.at[s, 0, c], z_peer(4, 1))]
-        if c == 0:
-            out.append(copy(zb.at[s, 0, 0], zb.at[s, 0, 0], zb_ss.at[s, 1], zb_rs.at[s, 1, 0], sibling(1)))
+        out = [copy(zb.at[s, c, 0], zb.at[s, c, 1], zb_ss.at[s], zb_rs.at[s, c], z_peer(4, 1))]
+        if c == 0:
+            out.append(copy(zb.at[s, 0, 0], zb.at[s, 0, 0], zb_ss.at[s], zb_rs.at[s, c], sibling(1)))
         return out
 
     def xb_copies(s):
         out = []
         for o in RING:
-            out.append(copy(xb.at[s], tb.at[s, x], xb_ss.at[s, o - 1, 0], xb_rs.at[s, o - 1], x_peer(o, 0)))
-            out.append(copy(tb.at[s, x], tb.at[s, x], xb_ss.at[s, o - 1, 1], xb_rs.at[s, o - 1], x_peer(o, 1)))
-        return out + [copy(xb.at[s], tb.at[s, x], xb_ss.at[s, 3, 0], xb_rs.at[s, 3], sibling(0))]
+            out.append(copy(xb.at[s], tb.at[s, x], xb_ss.at[s], xb_rs.at[s], x_peer(o, 0)))
+            out.append(copy(tb.at[s, x], tb.at[s, x], xb_ss.at[s], xb_rs.at[s], x_peer(o, 1)))
+        return out + [copy(xb.at[s], tb.at[s, x], xb_ss.at[s], xb_rs.at[s], sibling(0))]
 
     def sx_copies():
         out = [
-            copy(stx.at[x], stx.at[x], sx_ss.at[o - 1, c], sx_rs.at[o - 1], x_peer(o, c))
+            copy(stx.at[x], stx.at[x], sx_ss, sx_rs, x_peer(o, c))
             for o in RING for c in (0, 1)
         ]
-        return out + [copy(stx.at[x], stx.at[x], sx_ss.at[3, 0], sx_rs.at[3], sibling(0))]
+        return out + [copy(stx.at[x], stx.at[x], sx_ss, sx_rs, sibling(0))]
 
     def start(copies):
         for c in copies:
             c.start()
 
-    def sent(copies):
-        for c in copies:
-            c.wait_send()
-
-    def arrived(sems, like):
-        for r in sems:
-            pltpu.make_async_copy(like, like, r).wait()
+    def done(sem, like):
+        pltpu.make_async_copy(like, like, sem).wait()
 
     def by_core(f):
         pl.when(worker)(lambda: f(0))
         pl.when(hub)(lambda: f(1))
-
-    both = [(i, c) for i in range(3) for c in (0, 1)] + [(3, 0)]
 
     loads = [
         pltpu.make_async_copy(src, dst, in_sem.at[i])
@@ -361,7 +354,7 @@
         def _():
             @pl.when(first)
             def _():
-                arrived([ids_rs.at[i, c] for i, c in both], ids.at[0])
+                done(ids_rs, ids.at[0:7])
                 code = ids[0]
                 for p in range(1, 8):
                     code = code + ids[p]
@@ -376,27 +369,26 @@
                 pick[...] = full[:, :SEL].astype(BF16)
                 pickt[...] = full.T[:SEL].astype(BF16)
 
-            arrived([tab_rs.at[s, i, c] for i, c in both], tab.at[s, own])
+            done(tab_rs.at[s], tab.at[s, 0:7 * RB])
             selm[s] = two_term_pick(pickt[...], tab[s])
             start(sel_copies(s))
             rsel[s, y] = selm[s, mine]
 
-            arrived([cp_rs.at[s, i, c] for i, c in both], cparts.at[s, mine])
+            done(cp_rs.at[s], cparts.at[s, 0:56])
             dense[s] = two_term_pick(pick[...], cparts[s])
             start(dz_copies(s))
             rz[s, 3] = dense[s, own]
 
             @pl.when(last)
             def _():
-                arrived([ws_rs], wstat)
+                done(ws_rs, wstat)
                 add_share(s, dense[s] * tab[s])
                 add_share(s, uloc[0:RB] * rowband[...])
                 stz[z] = stat[...] + wstat[...]
                 for o in range(1, 8):
-                    copy(stz.at[z], stz.at[z], sz_ss.at[o - 1], sz_rs.at[o - 1], z_peer(o, 1)).start()
-
-        arrived([sel_rs.at[s, i] for i in range(3)], rsel.at[s, 0])
-        pl.when(worker)(lambda: arrived([sel_rs.at[s, 3]], rsel.at[s, 0]))
+                    copy(stz.at[z], stz.at[z], sz_ss, sz_rs, z_peer(o, 1)).start()
+
+        by_core(lambda c: done(sel_rs.at[s], rsel.at[s, 0:4 - c]))
         ucol = (rsel[s, 0] + rsel[s, 1]) + (rsel[s, 2] + rsel[s, 3])
         m2 = full_max(ucol)
         ucol = ucol * (1.0 / m2)
@@ -410,8 +402,7 @@
 
         pp_copy(s).wait_recv()
         total = total + jnp.where(iota16 == RB - 1, prevp[s], 0.0)
-        arrived([dz_rs.at[s, i] for i in range(3)], rz.at[s, 0])
-        pl.when(worker)(lambda: arrived([dz_rs.at[s, 3]], rz.at[s, 0]))
+        by_core(lambda c: done(dz_rs.at[s], rz.at[s, 0:4 - c]))
         total = total + ((rz[s, 0] + rz[s, 1]) + (rz[s, 2] + rz[s, 3]))
 
         zb[s, core, 0] = total[:, half:]
@@ -421,7 +412,10 @@
 
         @pl.when(worker)
         def _():
-            sent([*tab_copies(s, 0), up_copy(s), *cp_copies(s, 0), pp_copy(s)])
+            done(tab_ss.at[s], tab.at[s, 0:4 * RB])
+            done(cp_ss.at[s], cparts.at[s, 0:32])
+            up_copy(s).wait_send()
+            pp_copy(s).wait_send()
 
         @pl.when(hub)
         def _():
@@ -432,40 +426,51 @@
 
             @pl.when(last)
             def _():
-                for o in range(1, 8):
-                    copy(stz.at[z], stz.at[z], sz_ss.at[o - 1], sz_rs.at[o - 1], z_peer(o, 1)).wait()
+                done(sz_ss, stz.at[0:7])
+                done(sz_rs, stz.at[0:7])
                 v = stz[0]
                 for p in range(1, 8):
                     v = v + stz[p]
                 sty[y] = v
                 for o in RING:
-                    copy(sty.at[y], sty.at[y], sy_ss.at[o - 1], sy_rs.at[o - 1], y_peer(o, 1)).start()
-
-            sent([*tab_copies(s, 1), up_copy(s), *cp_copies(s, 1), pp_copy(s), *sel_copies(s), *dz_copies(s)])
-
-            arrived([xa_rs.at[s, i, c] for i, c in both], xa.at[s, 0, 0])
+                    copy(sty.at[y], sty.at[y], sy_ss, sy_rs, y_peer(o, 1)).start()
+
+            done(tab_ss.at[s], tab.at[s, 0:3 * RB])
+            done(cp_ss.at[s], cparts.at[s, 0:24])
+            up_copy(s).wait_send()
+            pp_copy(s).wait_send()
+            done(sel_ss.at[s], selm.at[s, 0:56])
+            done(dz_ss.at[s], dense.at[s, 0:7 * RB])
+
+            done(xa_rs.at[s, 0], xa.at[s, 0])
+            done(xa_rs.at[s, 1], xa.at[s, 1, 0:3])
             za[s] = (xa[s, 0, 0] + xa[s, 0, 1]) + (xa[s, 0, 2] + xa[s, 0, 3])
             ta[s, 0] = (xa[s, 1, 0] + xa[s, 1, 1]) + (xa[s, 1, 2] + xa[s, 1, 3])
             start(za_copies(s))
 
             @pl.when(last)
             def _():
-                for o in RING:
-                    copy(sty.at[y], sty.at[y], sy_ss.at[o - 1], sy_rs.at[o - 1], y_peer(o, 1)).wait()
+                done(sy_ss, sty.at[0:3])
+                done(sy_rs, sty.at[0:3])
                 stx[x] = (sty[0] + sty[1]) + (sty[2] + sty[3])
                 start(sx_copies())
 
-            arrived([zb_rs.at[s, 0, 0], zb_rs.at[s, 0, 1], zb_rs.at[s, 1, 0]], zb.at[s, 0, 0])
+            done(zb_rs.at[s, 0], zb.at[s, 0])
+            done(zb_rs.at[s, 1], zb.at[s, 1, 0])
             xb[s] = zb[s, 0, 0] + zb[s, 0, 1]
             tb[s, x] = zb[s, 1, 0] + zb[s, 1, 1]
             start(xb_copies(s))
 
-            sent([*za_copies(s), *xb_copies(s)])
-
-        by_core(lambda c: sent([*xa_copies(s, c), *zb_copies(s, c)]))
-        arrived([xb_rs.at[s, i] for i in range(3)], tb.at[s, 0])
-        pl.when(worker)(lambda: arrived([xb_rs.at[s, 3], za_rs.at[s, 0]], tb.at[s, 0]))
-        arrived([za_rs.at[s, 1]], tb.at[s, 0])
+            done(za_ss.at[s], xa.at[s, 0, 0:3])
+            done(xb_ss.at[s], selm.at[s, 0:56])
+
+        def rest(c):
+            done(xa_ss.at[s], xa.at[s, 0, 0:4 - c])
+            done(zb_ss.at[s], zb.at[s, 0, 0:2 - c])
+            done(xb_rs.at[s], tb.at[s, 0:4 - c])
+            done(za_rs.at[s], ta.at[s, 0:2 - c])
+
+        by_core(rest)
         tbuf[s + 1, :, :half] = ta[s, 0] + ta[s, 1]
         tbuf[s + 1, :, half:] = (tb[s, 0] + tb[s, 1]) + (tb[s, 2] + tb[s, 3])
 
@@ -473,17 +478,15 @@
 
     lax.fori_loop(0, SWEEPS, sweep, 0)
 
-    arrived([sx_rs.at[i] for i in range(3)], stx.at[0])
-
-    @pl.when(hub)
-    def _():
-        sent([*ids_copies(1), *sx_copies()])
-
-    @pl.when(worker)
-    def _():
-        sent([copy(stat, wstat, ws_ss, ws_rs, sibling(1)), *ids_copies(0)])
-        arrived([sx_rs.at[3]], stx.at[0])
-
+    def finish(c):
+        done(sx_rs, stx.at[0:4 - c])
+        done(ids_ss, ids.at[0:4 - c])
+        if c == 0:
+            done(ws_ss, stat)
+        else:
+            done(sx_ss, stz.at[0:7])
+
+    by_core(finish)
     v = (stx[0] + stx[1]) + (stx[2] + stx[3])
     count = v[0:1, 0:1] * 0.125
     mean1 = v[1:2, 0:1] * 2.0 / count
@@ -555,21 +558,21 @@
             vf(4, 8, 128),
             dma((4,)),
             dma((SLOTS,)),
-            dma((4,)), dma((4, 2)),
-            dma((S, 4)), dma((S, 4, 2)),
-            dma((S, 4, 2)), dma((S, 4)),
-            dma((S,)), dma((S,)),
-            dma((S, 4)), dma((S, 4, 2)),
-            dma((S,)), dma((S,)),
-            dma((S, 4, 2)), dma((S, 4)),
-            dma((S, 4)), dma((S, 4, 2)),
-            dma((S, 3)), dma((S, 2)),
-            dma((S, 2)), dma((S, 2, 2)),
-            dma((S, 4, 2)), dma((S, 4)),
             dma, dma,
-            dma((7,)), dma((7,)),
-            dma((3,)), dma((3,)),
-            dma((4, 2)), dma((4,)),
+            dma((S,)), dma((S,)),
+            dma((S,)), dma((S,)),
+            dma((S,)), dma((S,)),
+            dma((S,)), dma((S,)),
+            dma((S,)), dma((S,)),
+            dma((S,)), dma((S,)),
+            dma((S,)), dma((S, 2)),
+            dma((S,)), dma((S,)),
+            dma((S,)), dma((S, 2)),
+            dma((S,)), dma((S,)),
+            dma, dma,
+            dma, dma,
+            dma, dma,
+            dma, dma,
         ],
         compiler_params=pltpu.CompilerParams(
             collective_id=0, has_side_effects=True, vmem_limit_bytes=VMEM_LIMIT

time: 62.7 us -> 60.6 us (0.967)
  Pallas kernels: 59.9 us -> 57.7 us
    pallas_call x1, Pallas kernels: 59.9 us -> 57.7 us  [body(): pl.pallas_call(kernel, out_shape=out, in_specs=[hbm] * 5, out_specs=vm, s...]
where the time goes in v7:
time: 60.6 us; the launch traced here: 60.4 us
  Pallas kernels  57.7 us (95%)
  local copies, waits for them, and re-layouts  1.4 us (2%)
  between operations  1.28 us (2%)
    pallas_call x1, Pallas kernels, body(): pl.pallas_call(kernel, out_shape=out, in_specs=[hbm] * 5, out_specs=vm, s...  57.7 us
    reshape x1, local copies, waits for them, and re-layouts, body(): return (bias.reshape(seg), balance.reshape(seg))  1.4 us

profile of v7, /device:TPU:1, one launch (start us, length us, event | category | flops | bytes accessed | tf_op | source)
XLA Modules:
  0.0 60.4 jit_solution(4583167449302880539)
XLA Ops:
  1.3 57.7 %balance.1 = f32[128,128]{1,0:T(8,128)} custom-call(s32[12]{0:T(128)} %rows_hbm.1, s32[12]{0:T(128)} %cols_hbm.1, s32[1]{0:T(128)S(6)} %copy.7.cnt_hbm, s32[64,128]{1,0:T(8,128)} %bitcast.5, bf16[12,512,512]{2,1,0:T(8,128)(2,1)} %blocks_ref.1), custom_call_target="tpu_custom_call" | custom-call | tf_op jit(solution)/shard_map/balance/pallas_call | solution.py:517
  59.0 1.4 %slice_bitcast_fusion = (f32[8192]{0:T(1024)}, f32[8192]{0:T(1024)}) fusion(f32[128,128]{1,0:T(8,128)} %balance.1), kind=kLoop, calls=%fused_computation | loop fusion | bytes 131072 | tf_op jit(solution)/shard_map/reshape | solution.py:583

commit v8 on v7

--- a/solution.py
+++ b/solution.py
@@ -99,13 +99,13 @@
     own = seg(zl, core)
     mine = eight(yc)
 
-    def tab_copies(s, c):
+    def tab_copies(s, h, c):
         out = [
-            copy(tab.at[s, own], tab.at[s, own], tab_ss.at[s], tab_rs.at[s], z_peer(o, 1))
+            copy(tab.at[s, h, own], tab.at[s, h, own], tab_ss.at[s, h], tab_rs.at[s, h], z_peer(o, 1))
             for i, o in enumerate((two[c], 1, 7))
         ]
         if c == 0:
-            out.append(copy(tab.at[s, own], tab.at[s, own], tab_ss.at[s], tab_rs.at[s], sibling(1)))
+            out.append(copy(tab.at[s, h, own], tab.at[s, h, own], tab_ss.at[s, h], tab_rs.at[s, h], sibling(1)))
         return out
 
     def ids_copies(c):
@@ -129,13 +129,15 @@
     def pp_copy(s):
         return copy(pprev.at[s], prevp.at[s], pp_ss.at[s], pp_rs.at[s], step_peer(7))
 
-    def sel_copies(s):
+    def sel_copies(s, h):
         out = [
-            copy(selm.at[s, eight(lax.rem(y + o, 4) * 2 + c)], rsel.at[s, y],
-                 sel_ss.at[s], sel_rs.at[s], y_peer(o, c))
+            copy(selm.at[s, h, eight(lax.rem(y + o, 4) * 2 + c)], rsel.at[s, h, y],
+                 sel_ss.at[s, h], sel_rs.at[s, h], y_peer(o, c))
             for o in RING for c in (0, 1)
         ]
-        return out + [copy(selm.at[s, eight(y * 2)], rsel.at[s, y], sel_ss.at[s], sel_rs.at[s], sibling(0))]
+        return out + [
+            copy(selm.at[s, h, eight(y * 2)], rsel.at[s, h, y], sel_ss.at[s, h], sel_rs.at[s, h], sibling(0))
+        ]
 
     def dz_copies(s):
         out = [
@@ -147,11 +149,11 @@
 
     def xa_copies(s, c):
         out = [
-            copy(xa.at[s, c, x], xa.at[s, c, x], xa_ss.at[s], xa_rs.at[s, c], x_peer(o, 1))
+            copy(xa.at[s, c, x], xa.at[s, c, x], xa_ss.at[s], xa_rs.at[s], x_peer(o, 1))
             for o in RING
         ]
         if c == 0:
-            out.append(copy(xa.at[s, 0, x], xa.at[s, 0, x], xa_ss.at[s], xa_rs.at[s, c], sibling(1)))
+            out.append(copy(xa.at[s, 0, x], xa.at[s, 0, x], xa_ss.at[s], xa_rs.at[s], sibling(1)))
         return out
 
     def za_copies(s):
@@ -162,9 +164,9 @@
         ]
 
     def zb_copies(s, c):
-        out = [copy(zb.at[s, c, 0], zb.at[s, c, 1], zb_ss.at[s], zb_rs.at[s, c], z_peer(4, 1))]
+        out = [copy(zb.at[s, c, 0], zb.at[s, c, 1], zb_ss.at[s], zb_rs.at[s], z_peer(4, 1))]
         if c == 0:
-            out.append(copy(zb.at[s, 0, 0], zb.at[s, 0, 0], zb_ss.at[s], zb_rs.at[s, c], sibling(1)))
+            out.append(copy(zb.at[s, 0, 0], zb.at[s, 0, 0], zb_ss.at[s], zb_rs.at[s], sibling(1)))
         return out
 
     def xb_copies(s):
@@ -257,12 +259,15 @@
     def add_share(s, v):
         stat[...] += jnp.where(sub == s + 1, total_of(v), 0.0)
 
-    def weights(s):
-        u = jnp.where(keep[...] > 0, 4.0 / tbuf[s], 0.0)
-        ubuf[s] = u
-        tab[s, own] = u
-        uloc[0:RB] = u
-        ulast[s] = u[RB - 1:]
+    def weights(s, h, send=True):
+        lanes = slice(h * half, (h + 1) * half)
+        u = jnp.where(keep[:, lanes] > 0, 4.0 / tbuf[s, :, lanes], 0.0)
+        tab[s, h, own] = u
+        if send:
+            by_core(lambda c: start(tab_copies(s, h, c)))
+        ubuf[s, :, lanes] = u
+        uloc[0:RB, lanes] = u
+        ulast[s, :, lanes] = u[RB - 1:]
 
     def inter_columns(s):
         m = full_max(uloc[0:RB])
@@ -297,19 +302,18 @@
 
         lax.fori_loop(0, IR_MAX, one, 0)
 
+    weights(0, 0, send=False)
+    weights(0, 1, send=False)
+
     def open_up(c):
         pl.semaphore_wait(barrier, len(greet(c)))
-        start(ids_copies(c))
+        start([*tab_copies(0, 0, c), *tab_copies(0, 1, c), up_copy(0), *ids_copies(c)])
 
     by_core(open_up)
 
     def sweep(s, carry):
         first = s == 0
         last = s == SWEEPS - 1
-
-        weights(s)
-        by_core(lambda c: start(tab_copies(s, c)))
-        up_copy(s).start()
 
         @pl.when(first)
         def _():
@@ -330,25 +334,12 @@
 
         up_copy(s).wait_recv()
         uloc[RB:RB + 1] = uprev[s]
-        m = full_max(uloc[...])
-        inv = 1.0 / m
-        acc = None
-        for k in range(BAND):
-            vec = uloc[pl.ds(jnp.where(here[k], col_l[k], RB), 1), :] * inv
-            lhs = split2(jnp.where(iota16 == row_l[k], vec, 0.0))
-            part = lax.dot_general(
-                lhs, blk[k], (((1,), (1,)), ((), ())), preferred_element_type=F32
-            )
-            acc = part if acc is None else acc + part
-        rowband[...] = (acc[:RB] + acc[RB:]) * m
-
-        @pl.when(worker)
+        add_share(s, uloc[0:RB] * colband[...])
+        add_share(s, uprev[s] * pprev[s])
+
+        @pl.when(worker & last)
         def _():
-            add_share(s, uloc[0:RB] * rowband[...])
-
-            @pl.when(last)
-            def _():
-                copy(stat, wstat, ws_ss, ws_rs, sibling(1)).start()
+            copy(stat, wstat, ws_ss, ws_rs, sibling(1)).start()
 
         @pl.when(hub)
         def _():
@@ -369,10 +360,11 @@
                 pick[...] = full[:, :SEL].astype(BF16)
                 pickt[...] = full.T[:SEL].astype(BF16)
 
-            done(tab_rs.at[s], tab.at[s, 0:7 * RB])
-            selm[s] = two_term_pick(pickt[...], tab[s])
-            start(sel_copies(s))
-            rsel[s, y] = selm[s, mine]
+            for h in (0, 1):
+                done(tab_rs.at[s, h], tab.at[s, h, 0:7 * RB])
+                selm[s, h] = two_term_pick(pickt[...], tab[s, h])
+                start(sel_copies(s, h))
+                rsel[s, h, y] = selm[s, h, mine]
 
             done(cp_rs.at[s], cparts.at[s, 0:56])
             dense[s] = two_term_pick(pick[...], cparts[s])
@@ -382,26 +374,40 @@
             @pl.when(last)
             def _():
                 done(ws_rs, wstat)
-                add_share(s, dense[s] * tab[s])
-                add_share(s, uloc[0:RB] * rowband[...])
+                add_share(s, dense[s, :, :half] * tab[s, 0] + dense[s, :, half:] * tab[s, 1])
                 stz[z] = stat[...] + wstat[...]
                 for o in range(1, 8):
                     copy(stz.at[z], stz.at[z], sz_ss, sz_rs, z_peer(o, 1)).start()
 
-        by_core(lambda c: done(sel_rs.at[s], rsel.at[s, 0:4 - c]))
-        ucol = (rsel[s, 0] + rsel[s, 1]) + (rsel[s, 2] + rsel[s, 3])
-        m2 = full_max(ucol)
-        ucol = ucol * (1.0 / m2)
+        m = full_max(uloc[...])
+        inv = 1.0 / m
         acc = None
-        for k in range(IR_MAX):
-            target = jnp.where(k < live, row_l[BAND + k], -1)
-            lhs = split2(jnp.where(iota16 == target, ucol[k:k + 1], 0.0))
-            part = jnp.dot(lhs, blkt[k], preferred_element_type=F32)
+        for k in range(BAND):
+            vec = uloc[pl.ds(jnp.where(here[k], col_l[k], RB), 1), :] * inv
+            lhs = split2(jnp.where(iota16 == row_l[k], vec, 0.0))
+            part = lax.dot_general(
+                lhs, blk[k], (((1,), (1,)), ((), ())), preferred_element_type=F32
+            )
             acc = part if acc is None else acc + part
-        total = (acc[:RB] + acc[RB:]) * m2 + rowband[...] + colband[...]
+        rowband[...] = (acc[:RB] + acc[RB:]) * m
+
+        total = rowband[...] + colband[...]
+        for h in (0, 1):
+            by_core(lambda c, h=h: done(sel_rs.at[s, h], rsel.at[s, h, 0:4 - c]))
+            ucol = (rsel[s, h, 0] + rsel[s, h, 1]) + (rsel[s, h, 2] + rsel[s, h, 3])
+            m2 = full_max(ucol)
+            ucol = ucol * (1.0 / m2)
+            acc = None
+            for k in range(IR_MAX):
+                target = jnp.where(k < live, row_l[BAND + k], -1)
+                lhs = split2(jnp.where(iota16[:, :half] == target, ucol[k:k + 1], 0.0))
+                part = jnp.dot(lhs, blkt[k, h * half:(h + 1) * half, :], preferred_element_type=F32)
+                acc = part if acc is None else acc + part
+            total = total + (acc[:RB] + acc[RB:]) * m2
 
         pp_copy(s).wait_recv()
         total = total + jnp.where(iota16 == RB - 1, prevp[s], 0.0)
+
         by_core(lambda c: done(dz_rs.at[s], rz.at[s, 0:4 - c]))
         total = total + ((rz[s, 0] + rz[s, 1]) + (rz[s, 2] + rz[s, 3]))
 
@@ -412,7 +418,8 @@
 
         @pl.when(worker)
         def _():
-            done(tab_ss.at[s], tab.at[s, 0:4 * RB])
+            for h in (0, 1):
+                done(tab_ss.at[s, h], tab.at[s, h, 0:4 * RB])
             done(cp_ss.at[s], cparts.at[s, 0:32])
             up_copy(s).wait_send()
             pp_copy(s).wait_send()
@@ -421,8 +428,7 @@
         def _():
             @pl.when(jnp.logical_not(last))
             def _():
-                add_share(s, dense[s] * tab[s])
-                add_share(s, uloc[0:RB] * rowband[...])
+                add_share(s, dense[s, :, :half] * tab[s, 0] + dense[s, :, half:] * tab[s, 1])
 
             @pl.when(last)
             def _():
@@ -435,15 +441,15 @@
                 for o in RING:
                     copy(sty.at[y], sty.at[y], sy_ss, sy_rs, y_peer(o, 1)).start()
 
-            done(tab_ss.at[s], tab.at[s, 0:3 * RB])
+            for h in (0, 1):
+                done(tab_ss.at[s, h], tab.at[s, h, 0:3 * RB])
+                done(sel_ss.at[s, h], selm.at[s, h, 0:56])
             done(cp_ss.at[s], cparts.at[s, 0:24])
+            done(dz_ss.at[s], dense.at[s, 0:7 * RB])
             up_copy(s).wait_send()
             pp_copy(s).wait_send()
-            done(sel_ss.at[s], selm.at[s, 0:56])
-            done(dz_ss.at[s], dense.at[s, 0:7 * RB])
-
-            done(xa_rs.at[s, 0], xa.at[s, 0])
-            done(xa_rs.at[s, 1], xa.at[s, 1, 0:3])
+
+            done(xa_rs.at[s], dense.at[s, 0:56])
             za[s] = (xa[s, 0, 0] + xa[s, 0, 1]) + (xa[s, 0, 2] + xa[s, 0, 3])
             ta[s, 0] = (xa[s, 1, 0] + xa[s, 1, 1]) + (xa[s, 1, 2] + xa[s, 1, 3])
             start(za_copies(s))
@@ -455,24 +461,30 @@
                 stx[x] = (sty[0] + sty[1]) + (sty[2] + sty[3])
                 start(sx_copies())
 
-            done(zb_rs.at[s, 0], zb.at[s, 0])
-            done(zb_rs.at[s, 1], zb.at[s, 1, 0])
+            done(zb_rs.at[s], dense.at[s, 0:24])
             xb[s] = zb[s, 0, 0] + zb[s, 0, 1]
             tb[s, x] = zb[s, 1, 0] + zb[s, 1, 1]
             start(xb_copies(s))
 
-            done(za_ss.at[s], xa.at[s, 0, 0:3])
-            done(xb_ss.at[s], selm.at[s, 0:56])
+            done(za_ss.at[s], dense.at[s, 0:24])
+            done(xb_ss.at[s], dense.at[s, 0:56])
 
         def rest(c):
             done(xa_ss.at[s], xa.at[s, 0, 0:4 - c])
             done(zb_ss.at[s], zb.at[s, 0, 0:2 - c])
-            done(xb_rs.at[s], tb.at[s, 0:4 - c])
             done(za_rs.at[s], ta.at[s, 0:2 - c])
 
         by_core(rest)
-        tbuf[s + 1, :, :half] = ta[s, 0] + ta[s, 1]
-        tbuf[s + 1, :, half:] = (tb[s, 0] + tb[s, 1]) + (tb[s, 2] + tb[s, 3])
+        n = s + 1
+        tbuf[n, :, :half] = ta[s, 0] + ta[s, 1]
+        pl.when(jnp.logical_not(last))(lambda: weights(n, 0))
+        by_core(lambda c: done(xb_rs.at[s], tb.at[s, 0:4 - c]))
+        tbuf[n, :, half:] = (tb[s, 0] + tb[s, 1]) + (tb[s, 2] + tb[s, 3])
+
+        @pl.when(jnp.logical_not(last))
+        def _():
+            weights(n, 1)
+            up_copy(n).start()
 
         return carry
 
@@ -536,9 +548,9 @@
             vf(8, 128),
             vf(RB, BS),
             vf(RB, BS),
-            vf(S, 128, BS),
-            vf(S, SEL, BS),
-            vf(S, 4, 8, BS),
+            vf(S, 2, 128, H),
+            vf(S, 2, SEL, H),
+            vf(S, 2, 4, 8, H),
             vf(S, 1, BS),
             vf(S, 1, BS),
             vf(S, SEL, BS),
@@ -559,15 +571,15 @@
             dma((4,)),
             dma((SLOTS,)),
             dma, dma,
-            dma((S,)), dma((S,)),
-            dma((S,)), dma((S,)),
-            dma((S,)), dma((S,)),
-            dma((S,)), dma((S,)),
-            dma((S,)), dma((S,)),
-            dma((S,)), dma((S,)),
-            dma((S,)), dma((S, 2)),
-            dma((S,)), dma((S,)),
-            dma((S,)), dma((S, 2)),
+            dma((S, 2)), dma((S, 2)),
+            dma((S, 2)), dma((S, 2)),
+            dma((S,)), dma((S,)),
+            dma((S,)), dma((S,)),
+            dma((S,)), dma((S,)),
+            dma((S,)), dma((S,)),
+            dma((S,)), dma((S,)),
+            dma((S,)), dma((S,)),
+            dma((S,)), dma((S,)),
             dma((S,)), dma((S,)),
             dma, dma,
             dma, dma,

time: 60.6 us -> 60.1 us (level)
  no operation moved by 1% of the time
where the time goes in v8:
time: 60.1 us; the launch traced here: 59.9 us
  Pallas kernels  57.2 us (95%)
  local copies, waits for them, and re-layouts  1.4 us (2%)
  between operations  1.28 us (2%)
    pallas_call x1, Pallas kernels, body(): pl.pallas_call(kernel, out_shape=out, in_specs=[hbm] * 5, out_specs=vm, s...  57.2 us
    reshape x1, local copies, waits for them, and re-layouts, body(): return (bias.reshape(seg), balance.reshape(seg))  1.4 us

profile of v8, /device:TPU:1, one launch (start us, length us, event | category | flops | bytes accessed | tf_op | source)
XLA Modules:
  0.0 59.9 jit_solution(17145804160190055963)
XLA Ops:
  1.3 57.2 %balance.1 = f32[128,128]{1,0:T(8,128)} custom-call(s32[12]{0:T(128)} %rows_hbm.1, s32[12]{0:T(128)} %cols_hbm.1, s32[1]{0:T(128)S(6)} %copy.7.cnt_hbm, s32[64,128]{1,0:T(8,128)} %bitcast.5, bf16[12,512,512]{2,1,0:T(8,128)(2,1)} %blocks_ref.1), custom_call_target="tpu_custom_call" | custom-call | tf_op jit(solution)/shard_map/balance/pallas_call | solution.py:529
  58.5 1.4 %slice_bitcast_fusion = (f32[8192]{0:T(1024)}, f32[8192]{0:T(1024)}) fusion(f32[128,128]{1,0:T(8,128)} %balance.1), kind=kLoop, calls=%fused_computation | loop fusion | bytes 131072 | tf_op jit(solution)/shard_map/reshape | solution.py:595

commit v9 on v8

--- a/solution.py
+++ b/solution.py
@@ -101,11 +101,11 @@
 
     def tab_copies(s, h, c):
         out = [
-            copy(tab.at[s, h, own], tab.at[s, h, own], tab_ss.at[s, h], tab_rs.at[s, h], z_peer(o, 1))
+            copy(tab.at[s, h, own], tab.at[s, h, own], tab_ss.at[h], tab_rs.at[s, h], z_peer(o, 1))
             for i, o in enumerate((two[c], 1, 7))
         ]
         if c == 0:
-            out.append(copy(tab.at[s, h, own], tab.at[s, h, own], tab_ss.at[s, h], tab_rs.at[s, h], sibling(1)))
+            out.append(copy(tab.at[s, h, own], tab.at[s, h, own], tab_ss.at[h], tab_rs.at[s, h], sibling(1)))
         return out
 
     def ids_copies(c):
@@ -116,65 +116,65 @@
 
     def cp_copies(s, c):
         out = [
-            copy(cparts.at[s, mine], cparts.at[s, mine], cp_ss.at[s], cp_rs.at[s], y_peer(o, 1))
+            copy(cparts.at[s, mine], cparts.at[s, mine], cp_ss, cp_rs.at[s], y_peer(o, 1))
             for o in RING
         ]
         if c == 0:
-            out.append(copy(cparts.at[s, mine], cparts.at[s, mine], cp_ss.at[s], cp_rs.at[s], sibling(1)))
+            out.append(copy(cparts.at[s, mine], cparts.at[s, mine], cp_ss, cp_rs.at[s], sibling(1)))
         return out
 
     def up_copy(s):
-        return copy(ulast.at[s], uprev.at[s], up_ss.at[s], up_rs.at[s], step_peer(1))
+        return copy(ulast.at[s], uprev.at[s], up_ss, up_rs.at[s], step_peer(1))
 
     def pp_copy(s):
-        return copy(pprev.at[s], prevp.at[s], pp_ss.at[s], pp_rs.at[s], step_peer(7))
+        return copy(pprev.at[s], prevp.at[s], pp_ss, pp_rs.at[s], step_peer(7))
 
     def sel_copies(s, h):
         out = [
             copy(selm.at[s, h, eight(lax.rem(y + o, 4) * 2 + c)], rsel.at[s, h, y],
-                 sel_ss.at[s, h], sel_rs.at[s, h], y_peer(o, c))
+                 sel_ss.at[h], sel_rs.at[s, h], y_peer(o, c))
             for o in RING for c in (0, 1)
         ]
         return out + [
-            copy(selm.at[s, h, eight(y * 2)], rsel.at[s, h, y], sel_ss.at[s, h], sel_rs.at[s, h], sibling(0))
+            copy(selm.at[s, h, eight(y * 2)], rsel.at[s, h, y], sel_ss.at[h], sel_rs.at[s, h], sibling(0))
         ]
 
     def dz_copies(s):
         out = [
             copy(dense.at[s, seg(lax.rem(zl + o, 4), c)], rz.at[s, i],
-                 dz_ss.at[s], dz_rs.at[s], z_peer(o, c))
+                 dz_ss, dz_rs.at[s], z_peer(o, c))
             for c in (0, 1) for i, o in enumerate((two[c], 1, 7))
         ]
-        return out + [copy(dense.at[s, seg(zl, 0)], rz.at[s, 3], dz_ss.at[s], dz_rs.at[s], sibling(0))]
+        return out + [copy(dense.at[s, seg(zl, 0)], rz.at[s, 3], dz_ss, dz_rs.at[s], sibling(0))]
 
     def xa_copies(s, c):
         out = [
-            copy(xa.at[s, c, x], xa.at[s, c, x], xa_ss.at[s], xa_rs.at[s], x_peer(o, 1))
+            copy(xa.at[s, c, x], xa.at[s, c, x], xa_ss, xa_rs.at[s], x_peer(o, 1))
             for o in RING
         ]
         if c == 0:
-            out.append(copy(xa.at[s, 0, x], xa.at[s, 0, x], xa_ss.at[s], xa_rs.at[s], sibling(1)))
+            out.append(copy(xa.at[s, 0, x], xa.at[s, 0, x], xa_ss, xa_rs.at[s], sibling(1)))
         return out
 
     def za_copies(s):
         return [
-            copy(za.at[s], ta.at[s, 1], za_ss.at[s], za_rs.at[s], z_peer(4, 0)),
-            copy(ta.at[s, 0], ta.at[s, 1], za_ss.at[s], za_rs.at[s], z_peer(4, 1)),
-            copy(za.at[s], ta.at[s, 0], za_ss.at[s], za_rs.at[s], sibling(0)),
+            copy(za.at[s], ta.at[s, 1], za_ss, za_rs.at[s], z_peer(4, 0)),
+            copy(ta.at[s, 0], ta.at[s, 1], za_ss, za_rs.at[s], z_peer(4, 1)),
+            copy(za.at[s], ta.at[s, 0], za_ss, za_rs.at[s], sibling(0)),
         ]
 
     def zb_copies(s, c):
-        out = [copy(zb.at[s, c, 0], zb.at[s, c, 1], zb_ss.at[s], zb_rs.at[s], z_peer(4, 1))]
+        out = [copy(zb.at[s, c, 0], zb.at[s, c, 1], zb_ss, zb_rs.at[s], z_peer(4, 1))]
         if c == 0:
-            out.append(copy(zb.at[s, 0, 0], zb.at[s, 0, 0], zb_ss.at[s], zb_rs.at[s], sibling(1)))
+            out.append(copy(zb.at[s, 0, 0], zb.at[s, 0, 0], zb_ss, zb_rs.at[s], sibling(1)))
         return out
 
     def xb_copies(s):
         out = []
         for o in RING:
-            out.append(copy(xb.at[s], tb.at[s, x], xb_ss.at[s], xb_rs.at[s], x_peer(o, 0)))
-            out.append(copy(tb.at[s, x], tb.at[s, x], xb_ss.at[s], xb_rs.at[s], x_peer(o, 1)))
-        return out + [copy(xb.at[s], tb.at[s, x], xb_ss.at[s], xb_rs.at[s], sibling(0))]
+            out.append(copy(xb.at[s], tb.at[s, x], xb_ss, xb_rs.at[s], x_peer(o, 0)))
+            out.append(copy(tb.at[s, x], tb.at[s, x], xb_ss, xb_rs.at[s], x_peer(o, 1)))
+        return out + [copy(xb.at[s], tb.at[s, x], xb_ss, xb_rs.at[s], sibling(0))]
 
     def sx_copies():
         out = [
@@ -200,7 +200,7 @@
             (rows_hbm, rows_ref), (cols_hbm, cols_ref), (cnt_hbm, cnt_ref), (mask_hbm, mask_ref),
         ))
     ] + [
-        pltpu.make_async_copy(blocks_ref.at[k], blk.at[k], blk_sem.at[k])
+        pltpu.make_async_copy(blocks_ref.at[k], blk.at[k], blk_sem.at[1 if k < BAND else 0])
         for k in (*range(BAND, SLOTS), *range(BAND))
     ]
     loads[3].start()
@@ -317,16 +317,14 @@
 
         @pl.when(first)
         def _():
-            for c in loads[4:4 + IR_MAX]:
-                c.wait()
+            done(blk_sem.at[0], blk.at[BAND:])
 
         inter_columns(s)
         by_core(lambda c: start(cp_copies(s, c)))
 
         @pl.when(first)
         def _():
-            for c in loads[4 + IR_MAX:]:
-                c.wait()
+            done(blk_sem.at[1], blk.at[:BAND])
 
         band_columns(s)
         pp_copy(s).start()
@@ -412,15 +410,14 @@
         total = total + ((rz[s, 0] + rz[s, 1]) + (rz[s, 2] + rz[s, 3]))
 
         zb[s, core, 0] = total[:, half:]
-        by_core(lambda c: start(zb_copies(s, c)))
         xa[s, core, x] = total[:, :half]
-        by_core(lambda c: start(xa_copies(s, c)))
+        by_core(lambda c: start([*xa_copies(s, c), *zb_copies(s, c)]))
 
         @pl.when(worker)
         def _():
             for h in (0, 1):
-                done(tab_ss.at[s, h], tab.at[s, h, 0:4 * RB])
-            done(cp_ss.at[s], cparts.at[s, 0:32])
+                done(tab_ss.at[h], tab.at[s, h, 0:4 * RB])
+            done(cp_ss, cparts.at[s, 0:32])
             up_copy(s).wait_send()
             pp_copy(s).wait_send()
 
@@ -442,10 +439,10 @@
                     copy(sty.at[y], sty.at[y], sy_ss, sy_rs, y_peer(o, 1)).start()
 
             for h in (0, 1):
-                done(tab_ss.at[s, h], tab.at[s, h, 0:3 * RB])
-                done(sel_ss.at[s, h], selm.at[s, h, 0:56])
-            done(cp_ss.at[s], cparts.at[s, 0:24])
-            done(dz_ss.at[s], dense.at[s, 0:7 * RB])
+                done(tab_ss.at[h], tab.at[s, h, 0:3 * RB])
+                done(sel_ss.at[h], selm.at[s, h, 0:56])
+            done(cp_ss, cparts.at[s, 0:24])
+            done(dz_ss, dense.at[s, 0:7 * RB])
             up_copy(s).wait_send()
             pp_copy(s).wait_send()
 
@@ -466,12 +463,12 @@
             tb[s, x] = zb[s, 1, 0] + zb[s, 1, 1]
             start(xb_copies(s))
 
-            done(za_ss.at[s], dense.at[s, 0:24])
-            done(xb_ss.at[s], dense.at[s, 0:56])
+            done(za_ss, dense.at[s, 0:24])
+            done(xb_ss, dense.at[s, 0:56])
 
         def rest(c):
-            done(xa_ss.at[s], xa.at[s, 0, 0:4 - c])
-            done(zb_ss.at[s], zb.at[s, 0, 0:2 - c])
+            done(xa_ss, xa.at[s, 0, 0:4 - c])
+            done(zb_ss, zb.at[s, 0, 0:2 - c])
             done(za_rs.at[s], ta.at[s, 0:2 - c])
 
         by_core(rest)
@@ -569,18 +566,18 @@
             vf(4, 8, 128),
             vf(4, 8, 128),
             dma((4,)),
-            dma((SLOTS,)),
+            dma((2,)),
             dma, dma,
-            dma((S, 2)), dma((S, 2)),
-            dma((S, 2)), dma((S, 2)),
-            dma((S,)), dma((S,)),
-            dma((S,)), dma((S,)),
-            dma((S,)), dma((S,)),
-            dma((S,)), dma((S,)),
-            dma((S,)), dma((S,)),
-            dma((S,)), dma((S,)),
-            dma((S,)), dma((S,)),
-            dma((S,)), dma((S,)),
+            dma((2,)), dma((S, 2)),
+            dma((2,)), dma((S, 2)),
+            dma, dma((S,)),
+            dma, dma((S,)),
+            dma, dma((S,)),
+            dma, dma((S,)),
+            dma, dma((S,)),
+            dma, dma((S,)),
+            dma, dma((S,)),
+            dma, dma((S,)),
             dma, dma,
             dma, dma,
             dma, dma,

time: 60.1 us -> 59.6 us (level)
  no operation moved by 1% of the time
where the time goes in v9:
time: 59.6 us; the launch traced here: 59.5 us
  Pallas kernels  56.8 us (95%)
  local copies, waits for them, and re-layouts  1.4 us (2%)
  between operations  1.28 us (2%)
    pallas_call x1, Pallas kernels, body(): pl.pallas_call(kernel, out_shape=out, in_specs=[hbm] * 5, out_specs=vm, s...  56.8 us
    reshape x1, local copies, waits for them, and re-layouts, body(): return (bias.reshape(seg), balance.reshape(seg))  1.4 us

profile of v9, /device:TPU:1, one launch (start us, length us, event | category | flops | bytes accessed | tf_op | source)
XLA Modules:
  0.0 59.5 jit_solution(879079412675582792)
XLA Ops:
  1.3 56.8 %balance.1 = f32[128,128]{1,0:T(8,128)} custom-call(s32[12]{0:T(128)} %rows_hbm.1, s32[12]{0:T(128)} %cols_hbm.1, s32[1]{0:T(128)S(6)} %copy.7.cnt_hbm, s32[64,128]{1,0:T(8,128)} %bitcast.5, bf16[12,512,512]{2,1,0:T(8,128)(2,1)} %blocks_ref.1), custom_call_target="tpu_custom_call" | custom-call | tf_op jit(solution)/shard_map/balance/pallas_call | solution.py:526
  58.1 1.4 %slice_bitcast_fusion = (f32[8192]{0:T(1024)}, f32[8192]{0:T(1024)}) fusion(f32[128,128]{1,0:T(8,128)} %balance.1), kind=kLoop, calls=%fused_computation | loop fusion | bytes 131072 | tf_op jit(solution)/shard_map/reshape | solution.py:592

commit v10 on v9

--- a/solution.py
+++ b/solution.py
@@ -99,13 +99,16 @@
     own = seg(zl, core)
     mine = eight(yc)
 
+    def turn(s):
+        return s % 2 if isinstance(s, int) else lax.rem(s, 2)
+
     def tab_copies(s, h, c):
         out = [
-            copy(tab.at[s, h, own], tab.at[s, h, own], tab_ss.at[h], tab_rs.at[s, h], z_peer(o, 1))
+            copy(tab.at[s, h, own], tab.at[s, h, own], tab_ss.at[h], tab_rs.at[turn(s), h], z_peer(o, 1))
             for i, o in enumerate((two[c], 1, 7))
         ]
         if c == 0:
-            out.append(copy(tab.at[s, h, own], tab.at[s, h, own], tab_ss.at[h], tab_rs.at[s, h], sibling(1)))
+            out.append(copy(tab.at[s, h, own], tab.at[s, h, own], tab_ss.at[h], tab_rs.at[turn(s), h], sibling(1)))
         return out
 
     def ids_copies(c):
@@ -116,65 +119,65 @@
 
     def cp_copies(s, c):
         out = [
-            copy(cparts.at[s, mine], cparts.at[s, mine], cp_ss, cp_rs.at[s], y_peer(o, 1))
+            copy(cparts.at[s, mine], cparts.at[s, mine], cp_ss, cp_rs.at[turn(s)], y_peer(o, 1))
             for o in RING
         ]
         if c == 0:
-            out.append(copy(cparts.at[s, mine], cparts.at[s, mine], cp_ss, cp_rs.at[s], sibling(1)))
+            out.append(copy(cparts.at[s, mine], cparts.at[s, mine], cp_ss, cp_rs.at[turn(s)], sibling(1)))
         return out
 
     def up_copy(s):
-        return copy(ulast.at[s], uprev.at[s], up_ss, up_rs.at[s], step_peer(1))
+        return copy(ulast.at[s], uprev.at[s], up_ss, up_rs.at[turn(s)], step_peer(1))
 
     def pp_copy(s):
-        return copy(pprev.at[s], prevp.at[s], pp_ss, pp_rs.at[s], step_peer(7))
+        return copy(pprev.at[s], prevp.at[s], pp_ss, pp_rs.at[turn(s)], step_peer(7))
 
     def sel_copies(s, h):
         out = [
             copy(selm.at[s, h, eight(lax.rem(y + o, 4) * 2 + c)], rsel.at[s, h, y],
-                 sel_ss.at[h], sel_rs.at[s, h], y_peer(o, c))
+                 sel_ss.at[h], sel_rs.at[turn(s), h], y_peer(o, c))
             for o in RING for c in (0, 1)
         ]
         return out + [
-            copy(selm.at[s, h, eight(y * 2)], rsel.at[s, h, y], sel_ss.at[h], sel_rs.at[s, h], sibling(0))
+            copy(selm.at[s, h, eight(y * 2)], rsel.at[s, h, y], sel_ss.at[h], sel_rs.at[turn(s), h], sibling(0))
         ]
 
     def dz_copies(s):
         out = [
             copy(dense.at[s, seg(lax.rem(zl + o, 4), c)], rz.at[s, i],
-                 dz_ss, dz_rs.at[s], z_peer(o, c))
+                 dz_ss, dz_rs.at[turn(s)], z_peer(o, c))
             for c in (0, 1) for i, o in enumerate((two[c], 1, 7))
         ]
-        return out + [copy(dense.at[s, seg(zl, 0)], rz.at[s, 3], dz_ss, dz_rs.at[s], sibling(0))]
+        return out + [copy(dense.at[s, seg(zl, 0)], rz.at[s, 3], dz_ss, dz_rs.at[turn(s)], sibling(0))]
 
     def xa_copies(s, c):
         out = [
-            copy(xa.at[s, c, x], xa.at[s, c, x], xa_ss, xa_rs.at[s], x_peer(o, 1))
+            copy(xa.at[s, c, x], xa.at[s, c, x], xa_ss, xa_rs.at[turn(s)], x_peer(o, 1))
             for o in RING
         ]
         if c == 0:
-            out.append(copy(xa.at[s, 0, x], xa.at[s, 0, x], xa_ss, xa_rs.at[s], sibling(1)))
+            out.append(copy(xa.at[s, 0, x], xa.at[s, 0, x], xa_ss, xa_rs.at[turn(s)], sibling(1)))
         return out
 
     def za_copies(s):
         return [
-            copy(za.at[s], ta.at[s, 1], za_ss, za_rs.at[s], z_peer(4, 0)),
-            copy(ta.at[s, 0], ta.at[s, 1], za_ss, za_rs.at[s], z_peer(4, 1)),
-            copy(za.at[s], ta.at[s, 0], za_ss, za_rs.at[s], sibling(0)),
+            copy(za.at[s], ta.at[s, 1], za_ss, za_rs.at[turn(s)], z_peer(4, 0)),
+            copy(ta.at[s, 0], ta.at[s, 1], za_ss, za_rs.at[turn(s)], z_peer(4, 1)),
+            copy(za.at[s], ta.at[s, 0], za_ss, za_rs.at[turn(s)], sibling(0)),
         ]
 
     def zb_copies(s, c):
-        out = [copy(zb.at[s, c, 0], zb.at[s, c, 1], zb_ss, zb_rs.at[s], z_peer(4, 1))]
+        out = [copy(zb.at[s, c, 0], zb.at[s, c, 1], zb_ss, zb_rs.at[turn(s)], z_peer(4, 1))]
         if c == 0:
-            out.append(copy(zb.at[s, 0, 0], zb.at[s, 0, 0], zb_ss, zb_rs.at[s], sibling(1)))
+            out.append(copy(zb.at[s, 0, 0], zb.at[s, 0, 0], zb_ss, zb_rs.at[turn(s)], sibling(1)))
         return out
 
     def xb_copies(s):
         out = []
         for o in RING:
-            out.append(copy(xb.at[s], tb.at[s, x], xb_ss, xb_rs.at[s], x_peer(o, 0)))
-            out.append(copy(tb.at[s, x], tb.at[s, x], xb_ss, xb_rs.at[s], x_peer(o, 1)))
-        return out + [copy(xb.at[s], tb.at[s, x], xb_ss, xb_rs.at[s], sibling(0))]
+            out.append(copy(xb.at[s], tb.at[s, x], xb_ss, xb_rs.at[turn(s)], x_peer(o, 0)))
+            out.append(copy(tb.at[s, x], tb.at[s, x], xb_ss, xb_rs.at[turn(s)], x_peer(o, 1)))
+        return out + [copy(xb.at[s], tb.at[s, x], xb_ss, xb_rs.at[turn(s)], sibling(0))]
 
     def sx_copies():
         out = [
@@ -359,12 +362,12 @@
                 pickt[...] = full.T[:SEL].astype(BF16)
 
             for h in (0, 1):
-                done(tab_rs.at[s, h], tab.at[s, h, 0:7 * RB])
+                done(tab_rs.at[turn(s), h], tab.at[s, h, 0:7 * RB])
                 selm[s, h] = two_term_pick(pickt[...], tab[s, h])
                 start(sel_copies(s, h))
                 rsel[s, h, y] = selm[s, h, mine]
 
-            done(cp_rs.at[s], cparts.at[s, 0:56])
+            done(cp_rs.at[turn(s)], cparts.at[s, 0:56])
             dense[s] = two_term_pick(pick[...], cparts[s])
             start(dz_copies(s))
             rz[s, 3] = dense[s, own]
@@ -391,7 +394,7 @@
 
         total = rowband[...] + colband[...]
         for h in (0, 1):
-            by_core(lambda c, h=h: done(sel_rs.at[s, h], rsel.at[s, h, 0:4 - c]))
+            by_core(lambda c, h=h: done(sel_rs.at[turn(s), h], rsel.at[s, h, 0:4 - c]))
             ucol = (rsel[s, h, 0] + rsel[s, h, 1]) + (rsel[s, h, 2] + rsel[s, h, 3])
             m2 = full_max(ucol)
             ucol = ucol * (1.0 / m2)
@@ -406,7 +409,7 @@
         pp_copy(s).wait_recv()
         total = total + jnp.where(iota16 == RB - 1, prevp[s], 0.0)
 
-        by_core(lambda c: done(dz_rs.at[s], rz.at[s, 0:4 - c]))
+        by_core(lambda c: done(dz_rs.at[turn(s)], rz.at[s, 0:4 - c]))
         total = total + ((rz[s, 0] + rz[s, 1]) + (rz[s, 2] + rz[s, 3]))
 
         zb[s, core, 0] = total[:, half:]
@@ -446,7 +449,7 @@
             up_copy(s).wait_send()
             pp_copy(s).wait_send()
 
-            done(xa_rs.at[s], dense.at[s, 0:56])
+            done(xa_rs.at[turn(s)], dense.at[s, 0:56])
             za[s] = (xa[s, 0, 0] + xa[s, 0, 1]) + (xa[s, 0, 2] + xa[s, 0, 3])
             ta[s, 0] = (xa[s, 1, 0] + xa[s, 1, 1]) + (xa[s, 1, 2] + xa[s, 1, 3])
             start(za_copies(s))
@@ -458,7 +461,7 @@
                 stx[x] = (sty[0] + sty[1]) + (sty[2] + sty[3])
                 start(sx_copies())
 
-            done(zb_rs.at[s], dense.at[s, 0:24])
+            done(zb_rs.at[turn(s)], dense.at[s, 0:24])
             xb[s] = zb[s, 0, 0] + zb[s, 0, 1]
             tb[s, x] = zb[s, 1, 0] + zb[s, 1, 1]
             start(xb_copies(s))
@@ -469,13 +472,13 @@
         def rest(c):
             done(xa_ss, xa.at[s, 0, 0:4 - c])
             done(zb_ss, zb.at[s, 0, 0:2 - c])
-            done(za_rs.at[s], ta.at[s, 0:2 - c])
+            done(za_rs.at[turn(s)], ta.at[s, 0:2 - c])
 
         by_core(rest)
         n = s + 1
         tbuf[n, :, :half] = ta[s, 0] + ta[s, 1]
         pl.when(jnp.logical_not(last))(lambda: weights(n, 0))
-        by_core(lambda c: done(xb_rs.at[s], tb.at[s, 0:4 - c]))
+        by_core(lambda c: done(xb_rs.at[turn(s)], tb.at[s, 0:4 - c]))
         tbuf[n, :, half:] = (tb[s, 0] + tb[s, 1]) + (tb[s, 2] + tb[s, 3])
 
         @pl.when(jnp.logical_not(last))
@@ -503,8 +506,8 @@
     mean3 = v[3:4, 0:1] * 2.0 / count
     scale = mean1 * mean2 * 0.0625 * mean3
     b3 = tbuf[SWEEPS]
-    bias = jnp.where(keep[...] > 0, b3 / scale, 1.0)
-    balance = b3 * ubuf[SWEEPS - 1] / mean3
+    bias = jnp.where(keep[...] > 0, b3 * (1.0 / scale), 1.0)
+    balance = b3 * ubuf[SWEEPS - 1] * (1.0 / mean3)
     for q in range(4):
         out_ref[pl.ds(q, RB, stride=4), :] = bias[:, q * 128:(q + 1) * 128]
         out_ref[pl.ds(4 * RB + q, RB, stride=4), :] = balance[:, q * 128:(q + 1) * 128]
@@ -568,16 +571,16 @@
             dma((4,)),
             dma((2,)),
             dma, dma,
-            dma((2,)), dma((S, 2)),
-            dma((2,)), dma((S, 2)),
-            dma, dma((S,)),
-            dma, dma((S,)),
-            dma, dma((S,)),
-            dma, dma((S,)),
-            dma, dma((S,)),
-            dma, dma((S,)),
-            dma, dma((S,)),
-            dma, dma((S,)),
+            dma((2,)), dma((2, 2)),
+            dma((2,)), dma((2, 2)),
+            dma, dma((2,)),
+            dma, dma((2,)),
+            dma, dma((2,)),
+            dma, dma((2,)),
+            dma, dma((2,)),
+            dma, dma((2,)),
+            dma, dma((2,)),
+            dma, dma((2,)),
             dma, dma,
             dma, dma,
             dma, dma,

time: 59.6 us -> 59.6 us (level)
  no operation moved by 1% of the time
where the time goes in v10:
time: 59.6 us; the launch traced here: 59.4 us
  Pallas kernels  56.7 us (95%)
  local copies, waits for them, and re-layouts  1.4 us (2%)
  between operations  1.28 us (2%)
    pallas_call x1, Pallas kernels, body(): pl.pallas_call(kernel, out_shape=out, in_specs=[hbm] * 5, out_specs=vm, s...  56.7 us
    reshape x1, local copies, waits for them, and re-layouts, body(): return (bias.reshape(seg), balance.reshape(seg))  1.4 us

profile of v10, /device:TPU:1, one launch (start us, length us, event | category | flops | bytes accessed | tf_op | source)
XLA Modules:
  0.0 59.4 jit_solution(10805112708789836839)
XLA Ops:
  1.3 56.7 %balance.1 = f32[128,128]{1,0:T(8,128)} custom-call(s32[12]{0:T(128)} %rows_hbm.1, s32[12]{0:T(128)} %cols_hbm.1, s32[1]{0:T(128)S(6)} %copy.7.cnt_hbm, s32[64,128]{1,0:T(8,128)} %bitcast.5, bf16[12,512,512]{2,1,0:T(8,128)(2,1)} %blocks_ref.1), custom_call_target="tpu_custom_call" | custom-call | tf_op jit(solution)/shard_map/balance/pallas_call | solution.py:529
  58.0 1.4 %slice_bitcast_fusion = (f32[8192]{0:T(1024)}, f32[8192]{0:T(1024)}) fusion(f32[128,128]{1,0:T(8,128)} %balance.1), kind=kLoop, calls=%fused_computation | loop fusion | bytes 131072 | tf_op jit(solution)/shard_map/reshape | solution.py:595

commit v11 on v10

--- a/solution.py
+++ b/solution.py
@@ -146,7 +146,7 @@
         out = [
             copy(dense.at[s, seg(lax.rem(zl + o, 4), c)], rz.at[s, i],
                  dz_ss, dz_rs.at[turn(s)], z_peer(o, c))
-            for c in (0, 1) for i, o in enumerate((two[c], 1, 7))
+            for i, offsets in enumerate((two, (1, 1), (7, 7))) for c, o in enumerate(offsets)
         ]
         return out + [copy(dense.at[s, seg(zl, 0)], rz.at[s, 3], dz_ss, dz_rs.at[turn(s)], sibling(0))]
 

time: 59.6 us -> 60.4 us (1.013)
  Pallas kernels: 56.7 us -> 57.5 us
    pallas_call x1, Pallas kernels: 56.7 us -> 57.5 us  [body(): pl.pallas_call(kernel, out_shape=out, in_specs=[hbm] * 5, out_specs=vm, s...]
where the time goes in v11:
time: 60.4 us; the launch traced here: 60.2 us
  Pallas kernels  57.5 us (95%)
  local copies, waits for them, and re-layouts  1.4 us (2%)
  between operations  1.28 us (2%)
    pallas_call x1, Pallas kernels, body(): pl.pallas_call(kernel, out_shape=out, in_specs=[hbm] * 5, out_specs=vm, s...  57.5 us
    reshape x1, local copies, waits for them, and re-layouts, body(): return (bias.reshape(seg), balance.reshape(seg))  1.4 us

profile of v11, /device:TPU:1, one launch (start us, length us, event | category | flops | bytes accessed | tf_op | source)
XLA Modules:
  0.0 60.2 jit_solution(16779802137891080598)
XLA Ops:
  1.3 57.5 %balance.1 = f32[128,128]{1,0:T(8,128)} custom-call(s32[12]{0:T(128)} %rows_hbm.1, s32[12]{0:T(128)} %cols_hbm.1, s32[1]{0:T(128)S(6)} %copy.7.cnt_hbm, s32[64,128]{1,0:T(8,128)} %bitcast.5, bf16[12,512,512]{2,1,0:T(8,128)(2,1)} %blocks_ref.1), custom_call_target="tpu_custom_call" | custom-call | tf_op jit(solution)/shard_map/balance/pallas_call | solution.py:529
  58.8 1.4 %slice_bitcast_fusion = (f32[8192]{0:T(1024)}, f32[8192]{0:T(1024)}) fusion(f32[128,128]{1,0:T(8,128)} %balance.1), kind=kLoop, calls=%fused_computation | loop fusion | bytes 131072 | tf_op jit(solution)/shard_map/reshape | solution.py:595
